TPU v7x, 32 devices: a whole 2x2x4 slice. The times are simulated.
32 devices in a mesh: groups: 2 (over y), seq: 4 (over z), heads: 4 (over x, core).
Axes of the slice: x: 2, y: 2, z: 4, core: 2. Of those that a mesh axis runs over, the one named last changes fastest.
Arguments:
- prompt_token_input: bfloat16 [8, 256, 4096], P('groups', 'heads', 'seq'), parts along dimension 0, may hold values from -6 to 6
- lengths: int32 [8], P('groups'), parts along dimension 0, may hold values from 1 to 256, 512 in all
- request_adapter_index: int32 [8], P('groups'), parts along dimension 0, may hold values from 0 to 7
- assignment: int32 [8], P('groups'), parts along dimension 0, may hold values from 0 to 3, each once
- encoder_gate_weight: bfloat16 [4096, 5120], P(None, 'seq'), may hold values from -0.09375 to 0.09375
- encoder_up_weight: bfloat16 [4096, 5120], P(None, 'seq'), may hold values from -0.09375 to 0.09375
- encoder_down_weight: bfloat16 [5120, 4096], P('seq'), may hold values from -0.125 to 0.125
- adapter_down_maps: bfloat16 [8, 4096, 16], replicated, may hold values from -0.09375 to 0.09375
- adapter_up_maps: bfloat16 [8, 16, 5120], P(None, None, 'seq'), may hold values from -1.5 to 1.5
- text_key_value_weight: bfloat16 [4096, 2, 3072], P('seq', None, 'heads'), may hold values from -0.09375 to 0.09375
- image_token_activations: bfloat16 [8, 1024, 3072], P(('groups', 'seq'), 'heads'), parts along dimension 0, may hold values from -6 to 6
- modulation: bfloat16 [8, 2, 3072], P(('groups', 'seq')), parts along dimension 0, may hold values from -2.5 to 2.5
- image_query_key_value_weight: bfloat16 [3072, 3, 3072], P('seq', None, 'heads'), may hold values from -0.109375 to 0.109375
- query_key_norm_gain: float32 [3, 24, 128], P(None, 'heads'), may hold values from 0.5 to 2.5
Outputs:
- attended: bfloat16 [8, 1024, 3072], P(('groups', 'seq'), None, 'heads'), parts along dimension 0
There are 2 independent parts, one for each index of `groups`. A program takes and returns all parts, laid end to end along the dimension named above; an argument that names none is the same for every part. Nothing has to cross between parts.
Inputs may be any that keep to these rules, and one draw needn't show every extreme that they name: `lengths`: the longest prompt has exactly 256 tokens. `assignment`: every image index is assigned exactly one request.
All inputs are finite; a program needn't handle non-finite values.
Results may differ from a plain program's by a relative error of at most 0.014.
Values may be sent and summed in bfloat16 or wider, within the bound.
A program may use at most 192 MiB of HBM per device.

v0:
```python
import math

import jax
import jax.numpy as jnp
from jax import lax
from jax.sharding import PartitionSpec as P

eps_norm = 1e-06
adapter_scale = 0.5
neg_fill = -1e30


def rms_rows(values):
    return values * lax.rsqrt(jnp.mean(values * values, axis=-1, keepdims=True) + eps_norm)


def attend(queries, image_keys, image_values, text_keys, text_values, live_mask):
    factor = 1.0 / math.sqrt(queries.shape[-1])
    image_scores = (
        jnp.einsum("qhd,khd->hqk", queries, image_keys, preferred_element_type=jnp.float32) * factor
    )
    text_scores = (
        jnp.einsum("qhd,khd->hqk", queries, text_keys, preferred_element_type=jnp.float32) * factor
    )
    text_scores = jnp.where(live_mask[None, None, :], text_scores, neg_fill)
    scores = jnp.concatenate([image_scores, text_scores], axis=2)
    row_max = jnp.max(scores, axis=2, keepdims=True)
    weights = jnp.exp(scores - row_max)
    shares = (weights / jnp.sum(weights, axis=2, keepdims=True)).astype(jnp.bfloat16)
    values = jnp.concatenate([image_values, text_values], axis=0)
    return jnp.einsum("hqk,khd->qhd", shares, values, preferred_element_type=jnp.float32).astype(
        jnp.bfloat16
    )


def fold_into(gathered, weight_piece):
    return jnp.dot(gathered, weight_piece, preferred_element_type=jnp.float32)


def local(
    prompt_token_input,
    lengths,
    request_adapter_index,
    assignment,
    encoder_gate_weight,
    encoder_up_weight,
    encoder_down_weight,
    adapter_down_maps,
    adapter_up_maps,
    text_key_value_weight,
    image_token_activations,
    modulation,
    image_query_key_value_weight,
    query_key_norm_gain,
):
    requests = prompt_token_input.shape[0]
    positions = prompt_token_input.shape[1]
    my_slot = lax.axis_index("seq")
    whole = lax.all_gather(prompt_token_input, "seq", axis=2, tiled=True)
    width = whole.shape[2]
    normed = rms_rows(whole.astype(jnp.float32)).astype(jnp.bfloat16)
    tenant_adapters = adapter_down_maps.shape[0]
    selected_adapter = (
        request_adapter_index[:, None] == jnp.arange(tenant_adapters, dtype=jnp.int32)[None, :]
    ).astype(jnp.bfloat16)
    selected_down_maps = jnp.einsum(
        "mn,nhi->mhi", selected_adapter, adapter_down_maps, preferred_element_type=jnp.float32
    ).astype(jnp.bfloat16)
    selected_up_maps = jnp.einsum(
        "zl,log->zog", selected_adapter, adapter_up_maps, preferred_element_type=jnp.float32
    ).astype(jnp.bfloat16)
    adapter_projected = jnp.einsum(
        "rpd,rdk->rpk", normed, selected_down_maps, preferred_element_type=jnp.float32
    ).astype(jnp.bfloat16)
    flattened = normed.reshape(requests * positions, width)
    gated_hidden = jnp.dot(
        flattened, encoder_gate_weight, preferred_element_type=jnp.float32
    ).reshape(requests, positions, -1)
    gated_hidden = gated_hidden + adapter_scale * jnp.einsum(
        "sqt,sti->sqi", adapter_projected, selected_up_maps, preferred_element_type=jnp.float32
    )
    up_proj = jnp.dot(flattened, encoder_up_weight, preferred_element_type=jnp.float32).reshape(
        requests, positions, -1
    )
    hidden = (jax.nn.gelu(gated_hidden, approximate=True) * up_proj).astype(jnp.bfloat16)
    slots = jnp.arange(requests, dtype=jnp.int32)
    prompt_order = jnp.sum(
        slots[None, :] * (assignment[None, :] == slots[:, None]).astype(jnp.int32), axis=1
    )
    source_row = prompt_order[my_slot]
    ordered = jnp.take(hidden, prompt_order, axis=0)
    summed = lax.psum_scatter(
        jnp.einsum(
            "rpf,fd->rpd", ordered, encoder_down_weight, preferred_element_type=jnp.float32
        ).astype(jnp.bfloat16),
        "seq",
        scatter_dimension=0,
        tiled=True,
    ).astype(jnp.float32)
    residual = lax.dynamic_slice_in_dim(whole, source_row, 1, 0).astype(jnp.float32)
    prompt = (summed + residual).astype(jnp.bfloat16)[0]
    live_length = lengths[source_row]
    rows_all = lax.all_gather(prompt, "heads", axis=0, tiled=True)
    text_count = rows_all.shape[0]
    heads_here = query_key_norm_gain.shape[1]
    head_dim = query_key_norm_gain.shape[2]
    kv_local = text_key_value_weight.reshape(text_key_value_weight.shape[0], -1)
    text_proj = fold_into(rows_all, lax.all_gather(kv_local, "seq", axis=0, tiled=True))
    text_proj = text_proj.reshape(text_count, 2, heads_here, head_dim)
    text_keys = (rms_rows(text_proj[:, 0]) * query_key_norm_gain[2]).astype(jnp.bfloat16)
    text_values = text_proj[:, 1].astype(jnp.bfloat16)
    pixels = image_token_activations[0].astype(jnp.float32)
    row_mean = jnp.mean(pixels, axis=-1, keepdims=True)
    centered = pixels - row_mean
    normal_rows = centered * lax.rsqrt(
        jnp.mean(centered * centered, axis=-1, keepdims=True) + eps_norm
    )
    shift_row = modulation[0, 0].astype(jnp.float32)
    scale_row = modulation[0, 1].astype(jnp.float32)
    modulated = (normal_rows * (1.0 + scale_row) + shift_row).astype(jnp.bfloat16)
    full_image = lax.all_gather(modulated, "heads", axis=0, tiled=True)
    image_count = full_image.shape[0]
    qkv_local = image_query_key_value_weight.reshape(image_query_key_value_weight.shape[0], -1)
    image_proj = fold_into(full_image, lax.all_gather(qkv_local, "seq", axis=0, tiled=True))
    image_proj = image_proj.reshape(image_count, 3, heads_here, head_dim)
    image_queries = (rms_rows(image_proj[:, 0]) * query_key_norm_gain[0]).astype(jnp.bfloat16)
    image_keys = (rms_rows(image_proj[:, 1]) * query_key_norm_gain[1]).astype(jnp.bfloat16)
    image_values = image_proj[:, 2].astype(jnp.bfloat16)
    live_mask = jnp.arange(text_count, dtype=jnp.int32) < live_length
    output = attend(image_queries, image_keys, image_values, text_keys, text_values, live_mask)
    return output.reshape(1, image_count, heads_here * head_dim)


def solution(mesh):
    return jax.shard_map(
        local,
        mesh=mesh,
        in_specs=(
            P("groups", "heads", "seq"),
            P("groups"),
            P("groups"),
            P("groups"),
            P(None, "seq"),
            P(None, "seq"),
            P("seq", None),
            P(),
            P(None, None, "seq"),
            P("seq", None, "heads"),
            P(("groups", "seq"), "heads", None),
            P(("groups", "seq"), None, None),
            P("seq", None, "heads"),
            P(None, "heads", None),
        ),
        out_specs=P(("groups", "seq"), None, "heads"),
        check_vma=False,
    )
```

profile of v0, /device:TPU:0, one launch (start us, length us, event | category | flops | bytes accessed | tf_op | source)
XLA Modules:
  0.0 738.5 jit_solution(14212551089255681009)
XLA Ops:
  6.5 0.0 copy-start
  6.5 0.0 all-gather.11.cloned.1.call-start
  6.5 0.7 all-gather.11.cloned.1.call-update
  7.3 0.0 reduce-scatter.2.cloned.1.call-start
  7.3 0.8 select_reduce_fusion
  8.1 1.3 convolution_convert_fusion.1
  9.4 0.0 copy-done
  9.4 2.7 convolution_convert_fusion
  12.2 45.4 %all-gather.11.cloned.1.call-done = bf16[4,64,4096]{2,1,0:T(8,128)(2,1)} async-done(((bf16[4,64,1024]{2,1,0:T(8,128)(2,1)}), bf16[4,64,4096]{2,1,0:T(8,128)(2,1)}) %all-gather.11.cloned.1.call-update) | async-done | bytes 2097168 | tf_op jit(solution)/shard_map/all_gather | solution.py:59
  57.6 2.1 fusion.12
  59.7 0.0 copy-start.4
  59.7 0.0 copy-start.5
  59.7 8.7 %fusion.7 = f32[4,64,1280]{2,1,0:T(8,128)} fusion(bf16[4096,1280]{1,0:T(8,128)(2,1)} %param.18, bf16[4,64,4096]{2,1,0:T(8,128)(2,1)} %all-gather.11.cloned.1.call-done, f32[4,64]{1,0:T(4,128)S(1)} %add_rsqrt_fusion.3), kind=kOutput, calls=%fused_computation.11 | convolution fusion | flops 2687500288 | bytes 13894656 | tf_op jit(solution)/shard_map/dot_general | solution.py:76
  68.4 0.0 copy-done.4
  68.4 0.0 copy-done.5
  68.4 3.6 fusion.49
  72.1 7.2 fusion.25
  79.3 1.4 gather_fusion
  80.8 8.5 %fusion.9 = bf16[4,64,4096]{2,1,0:T(8,128)(2,1)} fusion(bf16[1280,4096]{1,0:T(8,128)(2,1)} %param.20, bf16[4,64,1280]{2,1,0:T(8,128)(2,1)} %gather_fusion, pred[4]{0:T(512)(128)(4,1)S(1)} %compare_and_fusion), kind=kOutput, calls=%fused_computation.16 | convolution fusion | flops 2685730816 | bytes 13238276 | tf_op jit(solution)/shard_map/rpf,fd->rpd/dot_general | solution.py:93
  89.2 0.0 reduce-scatter.2.cloned.1.call-update
  89.2 0.0 all-gather.15.cloned.1.call-start
  89.3 0.6 dynamic_slice.9
  91.8 40.2 %reduce-scatter.2.cloned.1.call-done = bf16[1,64,4096]{2,1,0:T(8,128)(2,1)} async-done(((bf16[4,64,4096]{2,1,0:T(8,128)(2,1)}), bf16[1,64,4096]{2,1,0:T(8,128)(2,1)}) %reduce-scatter.2.cloned.1.call-update) | async-done | bytes 524304 | tf_op jit(solution)/shard_map/reduce_scatter | solution.py:92
  132.0 2.0 add_convert_fusion
  134.0 0.0 all-gather.15.cloned.1.call-update
  134.0 0.0 all-gather.13.cloned.1.call-start
  134.1 4.1 copy.51
  138.2 0.0 copy-start.3
  138.2 0.0 copy-start.6
  138.2 0.0 all-gather.13.cloned.1.call-update
  138.2 0.2 all-gather.7.cloned.1.call-start
  138.4 1.2 copy-done.3
  139.6 0.3 convert_reduce_fusion
  139.9 0.6 fusion.17
  140.5 0.0 copy-done.6
  140.6 1.9 fusion.20
  142.5 0.0 all-gather.7.cloned.1.call-update
  142.5 0.0 all-gather.9.cloned.1.call-start
  142.6 6.1 copy.31
  148.6 0.0 copy-start.8
  148.6 0.0 copy-start.7
  148.6 0.0 all-gather.9.cloned.1.call-update
  148.7 0.6 copy-done.8
  149.3 0.6 dynamic_slice.11
  149.9 0.6 iota_compare_fusion.2
  150.5 0.0 copy-done.7
  150.5 5.5 all-gather.15.cloned.1.call-done
  156.1 219.7 %all-gather.13.cloned.1.call-done = bf16[4096,1536]{1,0:T(8,128)(2,1)} async-done(((bf16[1024,1536]{1,0:T(8,128)(2,1)}), bf16[4096,1536]{1,0:T(8,128)(2,1)}) %all-gather.13.cloned.1.call-update) | async-done | bytes 12582928 | tf_op jit(solution)/shard_map/all_gather | solution.py:108
  375.8 8.5 %fusion.28 = f32[256,1536]{0,1:T(8,128)S(1)} fusion(bf16[4096,1536]{1,0:T(8,128)(2,1)} %all-gather.13.cloned.1.call-done, bf16[1,256,4096]{2,1,0:T(8,128)(2,1)} %all-gather.15.cloned.1.call-done), kind=kOutput, calls=%fused_computation.41 | convolution fusion | flops 3221225472 | bytes 16252928 | tf_op jit(solution)/shard_map/dot_general | solution.py:37
  384.4 0.1 multiply_reduce_fusion.2
  384.5 37.4 %all-gather.7.cloned.1.call-done = bf16[1024,3072]{1,0:T(8,128)(2,1)} async-done(((bf16[256,3072]{1,0:T(8,128)(2,1)}), bf16[1024,3072]{1,0:T(8,128)(2,1)}) %all-gather.7.cloned.1.call-update) | async-done | bytes 6291472 | tf_op jit(solution)/shard_map/all_gather | solution.py:121
  421.9 245.5 %all-gather.9.cloned.1.call-done = bf16[3072,2304]{0,1:T(8,128)(2,1)} async-done(((bf16[768,2304]{0,1:T(8,128)(2,1)}), bf16[3072,2304]{0,1:T(8,128)(2,1)}) %all-gather.9.cloned.1.call-update) | async-done | bytes 14155792 | tf_op jit(solution)/shard_map/all_gather | solution.py:124
  667.4 19.4 %fusion.77 = f32[1024,2304]{0,1:T(8,128)S(1)} fusion(bf16[1024,3072]{1,0:T(8,128)(2,1)} %all-gather.7.cloned.1.call-done, bf16[3072,2304]{0,1:T(8,128)(2,1)} %all-gather.9.cloned.1.call-done), kind=kOutput, calls=%fused_computation.103 | convolution fusion | flops 14495514624 | bytes 29884416 | tf_op jit(solution)/shard_map/dot_general | solution.py:37
  686.8 0.8 multiply_reduce_fusion
  687.7 0.2 fusion.40
  688.0 10.2 %fusion.75 = (f32[6,1024]{1,0:T(8,128)S(1)}, f32[6,1024,1024]{1,2,0:T(8,128)}) fusion(f32[1024,3,6,128]{0,3,2,1:T(8,128)S(1)} %bitcast.99, f32[6,128]{1,0:T(8,128)S(1)} %get-tuple-element.7, f32[1024,6]{0,1:T(8,128)S(1)} %add_rsqrt_fusion, f32[6,128]{1,0:T(8,128)S(1)} %get-tuple-element.8, f32[1024,6]{0,1:T(8,128)S(1)} %add_rsqrt_fusion.1), kind=kOutput, calls=%fused_computation.101 | convolution fusion | flops 1627908096 | bytes 31555584 | tf_op jit(solution)/shard_map/qhd,khd->hqk/dot_general | solution.py:20
  698.2 2.0 fusion.76
  700.1 0.0 copy-start.2
  700.2 2.7 copy-done.2
  702.9 11.5 %fusion.1 = f32[6,1024]{1,0:T(8,128)S(1)} fusion(f32[6,1024,256]{1,2,0:T(8,128)S(1)} %get-tuple-element.13, f32[6,1024,1024]{1,2,0:T(8,128)} %get-tuple-element.11, f32[6,1024]{1,0:T(8,128)S(1)} %reduce_max.22), kind=kLoop, calls=%fused_computation.4 | loop fusion | flops 23586816 | bytes 31506432 | tf_op jit(solution)/shard_map/reduce_sum | solution.py:29
  714.3 0.0 copy-start.1
  714.4 15.7 %fusion.33 = bf16[6,128,1024]{2,1,0:T(8,128)(2,1)S(1)} fusion(f32[6,1024,256]{1,2,0:T(8,128)} %copy-done.2, f32[6,1024,1024]{1,2,0:T(8,128)} %get-tuple-element.11, f32[6,1024]{1,0:T(8,128)S(1)} %fusion.1, f32[6,1024]{1,0:T(8,128)S(1)} %reduce_max.22, bf16[256,6,128]{0,2,1:T(8,128)(2,1)S(1)} %fusion.60, bf16[1024,6,128]{0,2,1:T(8,128)(2,1)S(1)} %fusion.40), kind=kOutput, calls=%fused_computation.47 | convolution fusion | flops 2049441792 | bytes 35045376 | tf_op jit(solution)/shard_map/hqk,khd->qhd/dot_general | solution.py:31
  730.1 1.6 copy.43
  731.6 0.0 copy-done.1
  (14 shorter events, 0.2 us)
Async XLA Ops:
  6.5 2.9 copy-start
  6.5 51.1 %all-gather.11.cloned.1.call-start = ((), (), s32[]{:S(2)}) async-start(), calls=%async_computation.3 | async-start | bytes 2621440 | tf_op jit(solution)/shard_map/all_gather | solution.py:59
  7.3 124.7 %reduce-scatter.2.cloned.1.call-start = ((), (), s32[]{:S(2)}) async-start(), calls=%async_computation.4 | async-start | bytes 2621440 | tf_op jit(solution)/shard_map/reduce_scatter | solution.py:92
  59.7 8.7 %copy-start.4 = (bf16[4,64,4096]{2,1,0:T(8,128)(2,1)S(1)}, bf16[4,64,4096]{2,1,0:T(8,128)(2,1)}, u32[]{:S(2)}) copy-start(bf16[4,64,4096]{2,1,0:T(8,128)(2,1)} %all-gather.11.cloned.1.call-done) | copy-start | bytes 6291460
  59.7 8.7 %copy-start.5 = (bf16[4,4096,16]{1,0,2:T(4,128)(2,1)S(1)}, bf16[4,4096,16]{1,0,2:T(4,128)(2,1)}, u32[]{:S(2)}) copy-start(bf16[4,4096,16]{1,0,2:T(4,128)(2,1)} %convolution_convert_fusion) | copy-start | bytes 1572868
  89.2 66.8 %all-gather.15.cloned.1.call-start = ((), (), s32[]{:S(2)}) async-start(), calls=%async_computation.6 | async-start | bytes 2621440 | tf_op jit(solution)/shard_map/all_gather | solution.py:103
  134.0 241.8 %all-gather.13.cloned.1.call-start = ((), (), s32[]{:S(2)}) async-start(), calls=%async_computation.5 | async-start | bytes 15728640 | tf_op jit(solution)/shard_map/all_gather | solution.py:108
  138.2 1.5 copy-start.3
  138.2 2.3 copy-start.6
  138.2 283.7 %all-gather.7.cloned.1.call-start = ((), (), s32[]{:S(2)}) async-start(), calls=%async_computation.1 | async-start | bytes 7864320 | tf_op jit(solution)/shard_map/all_gather | solution.py:121
  142.5 524.8 %all-gather.9.cloned.1.call-start = ((), (), s32[]{:S(2)}) async-start(), calls=%async_computation.2 | async-start | bytes 17694720 | tf_op jit(solution)/shard_map/all_gather | solution.py:124
  148.6 0.7 copy-start.8
  148.6 1.9 copy-start.7
  700.1 2.7 copy-start.2
  714.3 17.3 %copy-start.1 = (bf16[8,4096,16]{1,2,0:T(8,128)(2,1)S(1)}, bf16[8,4096,16]{1,2,0:T(8,128)(2,1)}, u32[]{:S(2)}) copy-start(bf16[8,4096,16]{1,2,0:T(8,128)(2,1)} %param.21) | copy-start | bytes 3145732
Sparse Core Ops, SparseCore 0:
  8.9 48.6 all-gather.10
  89.4 42.5 reduce-scatter.1
  134.1 21.8 all-gather.14
  157.6 218.2 all-gather.12
  377.3 44.5 all-gather.6
  423.4 243.9 all-gather.8
where the time goes:
time: 739 us; the launch traced here: 738 us
  waiting for transfers between devices  595 us (81%)
  matrix products  88 us (12%)
  other arithmetic  20.7 us (3%)
  local copies, waits for them, and re-layouts  19.2 us (3%)
  between operations  15.6 us (2%)
    all_gather x1, waiting for transfers between devices, local(): lax.all_gather(qkv_local, 'seq', axis=0, tiled=True)  245 us
    all_gather x1, waiting for transfers between devices, local(): lax.all_gather(kv_local, 'seq', axis=0, tiled=True)  220 us
    all_gather x1, waiting for transfers between devices, local(): whole = lax.all_gather(prompt_token_input, 'seq', axis=2, tiled=True)  45.4 us
    reduce_scatter x1, waiting for transfers between devices, local(): lax.psum_scatter(jnp.einsum('rpf,fd->rpd', ordered, encoder_down_weight,...  40.2 us
    all_gather x1, waiting for transfers between devices, local(): full_image = lax.all_gather(modulated, 'heads', axis=0, tiled=True)  37.4 us
    dot_general x2, matrix products, fold_into(): return jnp.dot(gathered, weight_piece, preferred_element_type=jnp.float32)  28 us
    dot_general x1, matrix products, attend(): jnp.einsum('hqk,khd->qhd', shares, values, preferred_element_type=jnp.flo...  15.7 us
  transfers between devices with their start and end apart: 6, of which 6 were waited for; matrix products, arithmetic and copies ran while one was open for 4% of the time, Pallas kernels for 0%

commit v1 on v0

v1 whole, which is shorter than its diff:
```python
import functools
import math

import jax
import jax.numpy as jnp
from jax import lax
from jax.experimental import pallas as pl
from jax.experimental.pallas import tpu as pltpu
from jax.sharding import PartitionSpec as P

eps_norm = 1e-06
adapter_scale = 0.5
neg_fill = -1e30


def rms_rows(values):
    return values * lax.rsqrt(jnp.mean(values * values, axis=-1, keepdims=True) + eps_norm)


def line_plan(count):
    plan = []
    for place in range(count):
        found = []
        for steps in range(1, count):
            pair = [(place + steps, "down"), (place - steps, "up")]
            if place >= count // 2:
                pair.reverse()
            found += [(source, way, steps) for source, way in pair if 0 <= source < count]
        plan.append(found)
    return plan


def chunk_product(tokens, weight):
    return [
        jnp.dot(tokens, weight[j], preferred_element_type=jnp.float32)
        for j in range(weight.shape[0])
    ]


def added(left, right):
    return [a + b for a, b in zip(left, right)]


def attention_kernel(
    live_ref, gain_ref, query_ref, key_ref, value_ref, text_key_ref, text_value_ref, out_ref,
    *, rows_per_step
):
    head_dim = query_ref.shape[1]
    factor = 1.0 / math.sqrt(head_dim)
    live = live_ref[0]
    image_keys = (rms_rows(key_ref[...]) * gain_ref[0, 1][None, :]).astype(jnp.bfloat16)
    text_keys = (
        rms_rows(text_key_ref[...].astype(jnp.float32)) * gain_ref[0, 2][None, :]
    ).astype(jnp.bfloat16)
    image_values = value_ref[...].astype(jnp.bfloat16)
    text_values = text_value_ref[...].astype(jnp.bfloat16)
    text_count = text_keys.shape[0]
    contract = (((1,), (1,)), ((), ()))
    for start in range(0, query_ref.shape[0], rows_per_step):
        rows = pl.ds(start, rows_per_step)
        queries = (rms_rows(query_ref[rows, :]) * gain_ref[0, 0][None, :]).astype(jnp.bfloat16)
        image_scores = lax.dot_general(
            queries, image_keys, contract, preferred_element_type=jnp.float32
        )
        text_scores = lax.dot_general(
            queries, text_keys, contract, preferred_element_type=jnp.float32
        )
        image_weights = jnp.exp(image_scores * factor)
        position = lax.broadcasted_iota(jnp.int32, (rows_per_step, text_count), 1)
        text_weights = jnp.where(position < live, jnp.exp(text_scores * factor), 0.0)
        total = jnp.sum(image_weights, axis=1, keepdims=True) + jnp.sum(
            text_weights, axis=1, keepdims=True
        )
        inverse = 1.0 / total
        attended = jnp.dot(
            (image_weights * inverse).astype(jnp.bfloat16),
            image_values,
            preferred_element_type=jnp.float32,
        ) + jnp.dot(
            (text_weights * inverse).astype(jnp.bfloat16),
            text_values,
            preferred_element_type=jnp.float32,
        )
        out_ref[rows, :] = attended.astype(out_ref.dtype)


def attention(live_length, gain, queries, keys, values, text):
    image_count, columns = queries.shape
    head_dim = gain.shape[2]
    heads_here = columns // head_dim
    text_count = text.shape[0]

    def image_block():
        return pl.BlockSpec((image_count, head_dim), lambda h: (0, h))

    rows_per_step = math.gcd(image_count, 256)
    pairs = image_count * (image_count + text_count) * heads_here
    return pl.pallas_call(
        functools.partial(attention_kernel, rows_per_step=rows_per_step),
        grid=(heads_here,),
        in_specs=[
            pl.BlockSpec(memory_space=pltpu.SMEM),
            pl.BlockSpec((1, 3, head_dim), lambda h: (h, 0, 0)),
            image_block(),
            image_block(),
            image_block(),
            pl.BlockSpec((text_count, head_dim), lambda h: (0, h)),
            pl.BlockSpec((text_count, head_dim), lambda h: (0, heads_here + h)),
        ],
        out_specs=image_block(),
        out_shape=jax.ShapeDtypeStruct((image_count, columns), jnp.bfloat16),
        compiler_params=pltpu.CompilerParams(vmem_limit_bytes=40 * 1024 * 1024),
        cost_estimate=pl.CostEstimate(
            flops=4 * pairs * head_dim,
            bytes_accessed=14 * image_count * columns + 4 * text_count * columns,
            transcendentals=pairs,
        ),
    )(live_length.reshape(1), gain.transpose(1, 0, 2), queries, keys, values, text, text)


def modulated_rows(image_token_activations, modulation):
    pixels = image_token_activations[0].astype(jnp.float32)
    row_mean = jnp.mean(pixels, axis=-1, keepdims=True)
    centered = pixels - row_mean
    normal_rows = centered * lax.rsqrt(
        jnp.mean(centered * centered, axis=-1, keepdims=True) + eps_norm
    )
    shift_row = modulation[0, 0].astype(jnp.float32)
    scale_row = modulation[0, 1].astype(jnp.float32)
    return (normal_rows * (1.0 + scale_row) + shift_row).astype(jnp.bfloat16)


def image_part(image_token_activations, modulation, image_weight):
    replicas = lax.axis_size("groups")
    count = lax.axis_size("seq")
    my_replica = lax.axis_index("groups")
    place = lax.axis_index("seq")
    modulated = modulated_rows(image_token_activations, modulation)
    full_image = lax.all_gather(modulated, "heads", axis=0, tiled=True)
    depth = image_weight.shape[0]
    share = depth // replicas
    own = image_weight.transpose(1, 0, 2)
    piece = lax.dynamic_slice_in_dim(own, my_replica * share, share, 1)

    def tokens_of(first, length):
        return lax.dynamic_slice_in_dim(full_image, first, length, 1)

    plan = line_plan(count)
    going_up = [(i, i + 1) for i in range(count - 1)]
    going_down = [(i + 1, i) for i in range(count - 1)]
    up, down = [piece], [piece]
    total = chunk_product(tokens_of(place * depth, depth), own)
    for step in range(1, count):
        up.append(lax.ppermute(up[-1], "seq", going_up))
        down.append(lax.ppermute(down[-1], "seq", going_down))
        choices = {}
        for here in range(count):
            source, way, steps = plan[here][step - 1]
            choices.setdefault((way, steps), []).append(here)
        chosen = None
        for (way, steps), places in choices.items():
            array = (up if way == "up" else down)[steps]
            if chosen is None:
                chosen = array
            else:
                here = functools.reduce(jnp.logical_or, [place == i for i in places])
                chosen = jnp.where(here, array, chosen)
        source = jnp.array([plan[here][step - 1][0] for here in range(count)], jnp.int32)[place]
        chosen = lax.optimization_barrier(chosen)
        total = added(
            total, chunk_product(tokens_of(source * depth + my_replica * share, share), chosen)
        )
        for turn in range(1, replicas):
            theirs = lax.ppermute(
                chosen, "groups", [((i + turn) % replicas, i) for i in range(replicas)]
            )
            replica = lax.rem(my_replica + turn, replicas)
            total = added(
                total, chunk_product(tokens_of(source * depth + replica * share, share), theirs)
            )
    return total


def local(
    prompt_token_input,
    lengths,
    request_adapter_index,
    assignment,
    encoder_gate_weight,
    encoder_up_weight,
    encoder_down_weight,
    adapter_down_maps,
    adapter_up_maps,
    text_key_value_weight,
    image_token_activations,
    modulation,
    image_query_key_value_weight,
    query_key_norm_gain,
):
    requests = prompt_token_input.shape[0]
    positions = prompt_token_input.shape[1]
    my_slot = lax.axis_index("seq")
    whole = lax.all_gather(prompt_token_input, "seq", axis=2, tiled=True)
    image_proj = image_part(image_token_activations, modulation, image_query_key_value_weight)
    width = whole.shape[2]
    normed = rms_rows(whole.astype(jnp.float32)).astype(jnp.bfloat16)
    tenant_adapters = adapter_down_maps.shape[0]
    selected_adapter = (
        request_adapter_index[:, None] == jnp.arange(tenant_adapters, dtype=jnp.int32)[None, :]
    ).astype(jnp.bfloat16)
    selected_down_maps = jnp.einsum(
        "mn,nhi->mhi", selected_adapter, adapter_down_maps, preferred_element_type=jnp.float32
    ).astype(jnp.bfloat16)
    selected_up_maps = jnp.einsum(
        "zl,log->zog", selected_adapter, adapter_up_maps, preferred_element_type=jnp.float32
    ).astype(jnp.bfloat16)
    adapter_projected = jnp.einsum(
        "rpd,rdk->rpk", normed, selected_down_maps, preferred_element_type=jnp.float32
    ).astype(jnp.bfloat16)
    flattened = normed.reshape(requests * positions, width)
    gated_hidden = jnp.dot(
        flattened, encoder_gate_weight, preferred_element_type=jnp.float32
    ).reshape(requests, positions, -1)
    gated_hidden = gated_hidden + adapter_scale * jnp.einsum(
        "sqt,sti->sqi", adapter_projected, selected_up_maps, preferred_element_type=jnp.float32
    )
    up_proj = jnp.dot(flattened, encoder_up_weight, preferred_element_type=jnp.float32).reshape(
        requests, positions, -1
    )
    hidden = (jax.nn.gelu(gated_hidden, approximate=True) * up_proj).astype(jnp.bfloat16)
    slots = jnp.arange(requests, dtype=jnp.int32)
    prompt_order = jnp.sum(
        slots[None, :] * (assignment[None, :] == slots[:, None]).astype(jnp.int32), axis=1
    )
    source_row = prompt_order[my_slot]
    live_length = lengths[source_row]
    partial = jnp.einsum(
        "rpf,fd->rpd", hidden, encoder_down_weight, preferred_element_type=jnp.float32
    ).astype(jnp.bfloat16)
    summed = lax.psum_scatter(partial, "seq", scatter_dimension=2, tiled=True)
    encoded = (
        summed.astype(jnp.float32) + prompt_token_input.astype(jnp.float32)
    ).astype(jnp.bfloat16)
    prompts = lax.all_gather(encoded, "heads", axis=1, tiled=True)
    text_count = prompts.shape[1]
    ordered = jnp.take(prompts, prompt_order, axis=0).reshape(requests * text_count, -1)
    text_partial = jnp.concatenate(
        [
            jnp.dot(
                ordered, text_key_value_weight[:, j], preferred_element_type=jnp.float32
            ).astype(jnp.bfloat16)
            for j in range(2)
        ],
        axis=1,
    ).reshape(requests, text_count, -1)
    text = lax.psum_scatter(text_partial, "seq", scatter_dimension=0, tiled=True)[0]
    output = attention(
        live_length, query_key_norm_gain, image_proj[0], image_proj[1], image_proj[2], text
    )
    return output[None]


def solution(mesh):
    return jax.shard_map(
        local,
        mesh=mesh,
        in_specs=(
            P("groups", "heads", "seq"),
            P("groups"),
            P("groups"),
            P("groups"),
            P(None, "seq"),
            P(None, "seq"),
            P("seq", None),
            P(),
            P(None, None, "seq"),
            P("seq", None, "heads"),
            P(("groups", "seq"), "heads", None),
            P(("groups", "seq"), None, None),
            P("seq", None, "heads"),
            P(None, "heads", None),
        ),
        out_specs=P(("groups", "seq"), None, "heads"),
        check_vma=False,
    )
```

time: 739 us -> 507 us (0.69)
  waiting for transfers between devices: 595 us -> 267 us
  matrix products: 88 us -> 121 us
  local copies, waits for them, and re-layouts: 19.2 us -> 43.9 us
  starting transfers between devices: 0.39 us -> 19.7 us
  Pallas kernels: 0 us -> 17.1 us
    all_gather x4 -> x2, waiting for transfers between devices: 508 us -> 0.01 us  [the longest x1 0.01 us: image_part(): full_image = lax.all_gather(modulated, 'heads', axis=0, tiled=True)]
    ppermute x0 -> x9, waiting for transfers between devices: none -> 220 us  [the longest x3 138 us: image_part(): up.append(lax.ppermute(up[-1], 'seq', going_up))]
    reduce_scatter x1 -> x2, waiting for transfers between devices: 40.2 us -> 0.01 us  [the longest x1 0.01 us: local(): summed = lax.psum_scatter(partial, 'seq', scatter_dimension=2, tiled=True)]
    dot_general x7 -> x24, matrix products: 71.6 us -> 104 us  [the longest x21 85 us: chunk_product(): jnp.dot(tokens, weight[j], preferred_element_type=jnp.float32)]
    ppermute x0 -> x9, starting transfers between devices: none -> 19.3 us  [the longest x3 11.8 us: image_part(): up.append(lax.ppermute(up[-1], 'seq', going_up))]
    pallas_call x0 -> x1, Pallas kernels: none -> 17.1 us  [attention(): pl.pallas_call(functools.partial(attention_kernel, rows_per_step=rows_per...]
    concatenate x0 -> x1, local copies, waits for them, and re-layouts: none -> 13.1 us  [local(): jnp.concatenate([jnp.dot(ordered, text_key_value_weight[:, j], preferred_...]
    reduce_sum x3 -> x2, other arithmetic: 12.3 us -> 0.85 us  [the longest x1 0.56 us: modulated_rows(): jnp.mean(centered * centered, axis=-1, keepdims=True) + eps_norm]
  transfers between devices with their start and end apart: 6 -> 14, of which waited for: 6 -> 8; matrix products, arithmetic and copies ran while one was open for 4% -> 23% of each run, Pallas kernels for 0% -> 0%
where the time goes in v1:
time: 507 us; the launch traced here: 502 us
  waiting for transfers between devices  267 us (53%)
  matrix products  121 us (24%)
  local copies, waits for them, and re-layouts  43.9 us (9%)
  starting transfers between devices  19.7 us (4%)
  between operations  19 us (4%)
  Pallas kernels  17.1 us (3%)
  other arithmetic  14.6 us (3%)
    ppermute x3, waiting for transfers between devices, image_part(): up.append(lax.ppermute(up[-1], 'seq', going_up))  138 us
    dot_general x21, matrix products, chunk_product(): jnp.dot(tokens, weight[j], preferred_element_type=jnp.float32)  85 us
    ppermute x3, waiting for transfers between devices, image_part(): lax.ppermute(chosen, 'groups', [((i + turn) % replicas, i) for i in range...  76.4 us
    all_gather x1, waiting for transfers between devices, local(): whole = lax.all_gather(prompt_token_input, 'seq', axis=2, tiled=True)  46.2 us
    pallas_call x1, Pallas kernels, attention(): pl.pallas_call(functools.partial(attention_kernel, rows_per_step=rows_per...  17.1 us
    dot_general x1, matrix products, local(): jnp.einsum('rpf,fd->rpd', hidden, encoder_down_weight, preferred_element_...  15.5 us
    unnamed x77, local copies, waits for them, and re-layouts  14.2 us
    concatenate x1, local copies, waits for them, and re-layouts, local(): jnp.concatenate([jnp.dot(ordered, text_key_value_weight[:, j], preferred_...  13.1 us
  transfers between devices with their start and end apart: 14, of which 8 were waited for; matrix products, arithmetic and copies ran while one was open for 23% of the time, Pallas kernels for 0%

profile of v1, /device:TPU:0, one launch (start us, length us, event | category | flops | bytes accessed | tf_op | source)
XLA Modules:
  0.0 502.0 jit_solution(6794112936057449602)
XLA Ops:
  8.1 1.3 convolution_convert_fusion.1
  9.4 2.8 convolution_convert_fusion
  12.2 46.2 %all-gather.6.cloned.1.call-done = bf16[4,64,4096]{2,1,0:T(8,128)(2,1)} async-done(((bf16[4,64,1024]{2,1,0:T(8,128)(2,1)}), bf16[4,64,4096]{2,1,0:T(8,128)(2,1)}) %all-gather.6.cloned.1.call-update) | async-done | bytes 2097168 | tf_op jit(solution)/shard_map/all_gather | solution.py:203
  58.4 2.1 fusion.9
  60.5 8.7 %fusion.4 = f32[4,64,1280]{2,1,0:T(8,128)} fusion(bf16[4096,1280]{1,0:T(8,128)(2,1)} %param.21, bf16[4,64,4096]{2,1,0:T(8,128)(2,1)} %all-gather.6.cloned.1.call-done, f32[4,64]{1,0:T(4,128)S(1)} %add_rsqrt_fusion), kind=kOutput, calls=%fused_computation.5 | convolution fusion | flops 2687500288 | bytes 13894656 | tf_op jit(solution)/shard_map/dot_general | solution.py:221
  69.3 3.6 fusion.39
  72.9 15.5 %fusion.6 = bf16[4,64,4096]{2,1,0:T(8,128)(2,1)} fusion(bf16[1280,4096]{1,0:T(8,128)(2,1)} %param.23, f32[4,64,1280]{2,1,0:T(8,128)} %fusion.39, bf16[4096,1280]{1,0:T(8,128)(2,1)} %param.22, bf16[4,64,4096]{2,1,0:T(8,128)(2,1)S(1)} %copy-done.23, f32[4,64]{1,0:T(4,128)S(1)} %add_rsqrt_fusion), kind=kOutput, calls=%fused_computation.9 | convolution fusion | flops 5373558784 | bytes 26477568 | tf_op jit(solution)/shard_map/rpf,fd->rpd/dot_general | solution.py:237
  88.8 1.1 copy-done.7
  90.8 1.9 fusion.17
  92.8 1.8 dynamic-slice_bitcast_fusion
  94.6 1.7 collective-permute-start
  96.3 1.3 collective-permute-start.1
  97.6 67.3 %collective-permute-done = bf16[3,384,768]{2,1,0:T(8,128)(2,1)S(1)} collective-permute-done((bf16[3,384,768]{2,1,0:T(8,128)(2,1)S(1)}, bf16[3,384,768]{2,1,0:T(8,128)(2,1)S(1)}, u32[]{:S(2)}, u32[]{:S(2)}) %collective-permute-start) | collective-permute-done | bytes 1769504 | tf_op jit(solution)/shard_map/ppermute | solution.py:154
  164.8 1.3 copy-done.24
  166.1 4.5 collective-permute-start.3
  170.6 1.3 collective-permute-start.4
  171.9 36.3 %collective-permute-done.3 = bf16[3,384,768]{2,1,0:T(8,128)(2,1)S(1)} collective-permute-done((bf16[3,384,768]{2,1,0:T(8,128)(2,1)S(1)}, bf16[3,384,768]{2,1,0:T(8,128)(2,1)S(1)}, u32[]{:S(2)}, u32[]{:S(2)}) %collective-permute-start.3) | collective-permute-done | bytes 1769504 | tf_op jit(solution)/shard_map/ppermute | solution.py:154
  208.3 5.6 %collective-permute-start.6 = (bf16[3,384,768]{2,1,0:T(8,128)(2,1)S(1)}, bf16[3,384,768]{2,1,0:T(8,128)(2,1)}, u32[]{:S(2)}, u32[]{:S(2)}) collective-permute-start(bf16[3,384,768]{2,1,0:T(8,128)(2,1)S(1)} %collective-permute-done.3), channel_id=1, source_target_pairs={{0,4},{4,8},{8,12},{1,5},{5,9},{9,13},{2,6},{6,10},{10,14},{3,7},{... | collective-permute-start | bytes 5308424 | tf_op jit(solution)/shard_map/ppermute | solution.py:154
  213.9 1.3 collective-permute-start.7
  215.3 34.4 %collective-permute-done.6 = bf16[3,384,768]{2,1,0:T(8,128)(2,1)} collective-permute-done((bf16[3,384,768]{2,1,0:T(8,128)(2,1)S(1)}, bf16[3,384,768]{2,1,0:T(8,128)(2,1)}, u32[]{:S(2)}, u32[]{:S(2)}) %collective-permute-start.6) | collective-permute-done | bytes 1769504 | tf_op jit(solution)/shard_map/ppermute | solution.py:154
  249.6 5.7 %collective-permute-done.7 = bf16[3,384,768]{2,1,0:T(8,128)(2,1)} collective-permute-done((bf16[3,384,768]{2,1,0:T(8,128)(2,1)}, bf16[3,384,768]{2,1,0:T(8,128)(2,1)}, u32[]{:S(2)}, u32[]{:S(2)}) %collective-permute-start.7) | collective-permute-done | bytes 1769504 | tf_op jit(solution)/shard_map/ppermute | solution.py:155
  255.3 5.2 %broadcast_select_fusion.1 = (bf16[3,384,768]{2,1,0:T(8,128)(2,1)}, bf16[3,384,768]{2,1,0:T(8,128)(2,1)}, bf16[3,384,768]{2,1,0:T(8,128)(2,1)S(1)}) fusion(bf16[3,384,768]{2,1,0:T(8,128)(2,1)} %copy-done.24, bf16[3,384,768]{2,1,0:T(8,128)(2,1)} %copy-done.25, pred[]{:T(512)S(6)} %or.3, bf16[3,384,768]{2,1,0:T(8,128)(2,1)} %copy-done.26, ...), kind=kLoop, calls=%fused_computation.36 | loop fusion | flops 6193152 | bytes 15925252 | tf_op jit(solution)/shard_map/jit(_where)/select_n | solution.py:167
  260.5 1.6 collective-permute-start.8
  269.7 2.1 add_convert_fusion
  271.8 9.4 %fusion.116 = (bf16[1024,1,768]{2,1,0:T(2,128)(2,1)}, bf16[1024,1,768]{2,1,0:T(2,128)(2,1)}) fusion(bf16[1024,2,768]{2,1,0:T(2,128)(2,1)} %param.26), kind=kLoop, calls=%fused_computation.153 | loop fusion | bytes 6291456 | tf_op jit(solution)/shard_map/slice | solution.py:250
  281.3 1.6 collective-permute-start.2
  282.9 19.4 %collective-permute-done.8 = bf16[3,384,768]{2,1,0:T(8,128)(2,1)} collective-permute-done((bf16[3,384,768]{2,1,0:T(8,128)(2,1)S(1)}, bf16[3,384,768]{2,1,0:T(8,128)(2,1)}, u32[]{:S(2)}, u32[]{:S(2)}) %collective-permute-start.8) | collective-permute-done | bytes 1769504 | tf_op jit(solution)/shard_map/ppermute | solution.py:174
  302.3 4.1 fusion.52
  306.4 4.0 fusion.54
  310.4 29.8 %collective-permute-done.5 = bf16[3,384,768]{2,1,0:T(8,128)(2,1)} collective-permute-done((bf16[3,384,768]{2,1,0:T(8,128)(2,1)}, bf16[3,384,768]{2,1,0:T(8,128)(2,1)}, u32[]{:S(2)}, u32[]{:S(2)}) %collective-permute-start.5) | collective-permute-done | bytes 1769504 | tf_op jit(solution)/shard_map/ppermute | solution.py:174
  340.2 3.8 fusion.61
  343.9 3.7 fusion.63
  347.6 27.2 %collective-permute-done.2 = bf16[3,384,768]{2,1,0:T(8,128)(2,1)} collective-permute-done((bf16[3,384,768]{2,1,0:T(8,128)(2,1)}, bf16[3,384,768]{2,1,0:T(8,128)(2,1)}, u32[]{:S(2)}, u32[]{:S(2)}) %collective-permute-start.2) | collective-permute-done | bytes 1769504 | tf_op jit(solution)/shard_map/ppermute | solution.py:174
  374.8 3.7 fusion.73
  378.5 3.7 fusion.75
  382.2 2.3 gather_fusion
  384.8 1.6 copy-done.21
  386.4 1.8 convolution_convert_fusion.2
  388.3 1.8 convolution_convert_fusion.3
  390.1 2.0 pad_maximum_fusion
  392.1 13.1 %copy.31 = bf16[1024,1536]{1,0:T(8,128)(2,1)} copy(bf16[1024,1536]{0,1:T(8,128)(2,1)} %pad_maximum_fusion) | data formatting | bytes 6291456 | tf_op jit(solution)/shard_map/concatenate | solution.py:247
  405.3 1.4 copy-done.19
  406.7 3.9 fusion.67
  410.7 4.1 fusion.69
  414.8 4.1 fusion.79
  418.8 3.7 fusion.81
  422.5 2.0 fusion.65
  424.6 3.7 fusion.77
  428.2 3.7 fusion.56
  432.0 2.6 fusion.71
  434.6 3.9 fusion.83
  438.4 3.1 fusion.40
  441.5 3.1 fusion.42
  444.6 3.1 fusion.44
  447.7 1.0 copy-done.12
  448.6 0.9 copy-done.13
  449.6 7.4 %add_add_fusion.value_ref = f32[1024,768]{1,0:T(8,128)} fusion(f32[1024,768]{1,0:T(8,128)S(1)} %copy-done.10, f32[1024,768]{1,0:T(8,128)S(1)} %copy-done.12, f32[1024,768]{1,0:T(8,128)} %fusion.67, f32[1024,768]{1,0:T(8,128)S(1)} %copy-done.13, f32[1024,768]{1,0:T(8,128)} %fusion.40, f32[1024,768]{1,0:T(8,128)} %fusion.79, ...), kind=kOutput, calls=%fused_computation.23 | convolution fusion | flops 608698368 | bytes 23396356 | tf_op jit(solution)/shard_map/dot_general | solution.py:35
  457.0 7.5 %add_add_fusion.1.key_ref = f32[1024,768]{1,0:T(8,128)} fusion(f32[1024,768]{1,0:T(8,128)S(1)} %copy-done.8, f32[1024,768]{1,0:T(8,128)S(1)} %copy-done.9, f32[1024,768]{1,0:T(8,128)} %fusion.69, f32[1024,768]{1,0:T(8,128)S(1)} %copy-done.11, f32[1024,768]{1,0:T(8,128)} %fusion.42, f32[1024,768]{1,0:T(8,128)} %fusion.81, ...), kind=kOutput, calls=%fused_computation.24 | convolution fusion | flops 608698368 | bytes 23396356 | tf_op jit(solution)/shard_map/dot_general | solution.py:35
  464.5 6.3 %add_add_fusion.2.query_ref = f32[1024,768]{1,0:T(8,128)} fusion(f32[1024,768]{1,0:T(8,128)S(1)} %copy-done.15, f32[1024,768]{1,0:T(8,128)S(1)} %fusion.65, f32[1024,768]{1,0:T(8,128)S(1)} %copy-done.16, f32[1024,768]{1,0:T(8,128)S(1)} %copy-done.14, f32[1024,768]{1,0:T(8,128)} %fusion.44, f32[1024,768]{1,0:T(8,128)} %fusion.83, ...), kind=kOutput, calls=%fused_computation.25 | convolution fusion | flops 608698368 | bytes 23396356 | tf_op jit(solution)/shard_map/dot_general | solution.py:35
  470.7 1.9 copy-done.2
  472.6 1.9 copy-done.3
  474.5 1.9 copy-done.4
  476.4 1.1 copy-done.5
  477.5 17.1 %shard_map.163 = bf16[1024,768]{1,0:T(8,128)(2,1)} custom-call(s32[1]{0:T(128)} %dynamic_slice.40.live_ref, f32[6,3,128]{2,1,0:T(4,128)S(1)} %bitcast.128, f32[1024,768]{1,0:T(8,128)S(1)} %copy-done.4, f32[1024,768]{1,0:T(8,128)S(1)} %copy-done.3, f32[1024,768]{1,0:T(8,128)S(1)} %copy-done.2, bf16[256,1536]{1,0:T(8,128)(2,1)S(1)} %bitcast.129, ...), custom_call_target="tpu_custom_call" | custom-call | flops 4026531840 | bytes 11796480 | tf_op jit(solution)/shard_map/pallas_call | solution.py:98
  (102 shorter events, 6.2 us)
Async XLA Ops:
  7.4 2.1 copy-start
  7.4 51.1 %all-gather.6.cloned.1.call-start = ((), (), s32[]{:S(2)}) async-start(), calls=%async_computation.3 | async-start | bytes 2621440 | tf_op jit(solution)/shard_map/all_gather | solution.py:203
  8.1 261.6 %reduce-scatter.3.cloned.1.call-start = ((), (), s32[]{:S(2)}) async-start(), calls=%async_computation.4 | async-start | bytes 2621440 | tf_op jit(solution)/shard_map/reduce_scatter | solution.py:240
  60.5 8.7 %copy-start.23 = (bf16[4,64,4096]{2,1,0:T(8,128)(2,1)S(1)}, bf16[4,64,4096]{2,1,0:T(8,128)(2,1)}, u32[]{:S(2)}) copy-start(bf16[4,64,4096]{2,1,0:T(8,128)(2,1)} %all-gather.6.cloned.1.call-done) | copy-start | bytes 6291460
  60.5 8.7 %copy-start.28 = (bf16[4,4096,16]{1,0,2:T(4,128)(2,1)S(1)}, bf16[4,4096,16]{1,0,2:T(4,128)(2,1)}, u32[]{:S(2)}) copy-start(bf16[4,4096,16]{1,0,2:T(4,128)(2,1)} %convolution_convert_fusion) | copy-start | bytes 1572868
  88.5 1.4 copy-start.7
  88.5 2.3 copy-start.29
  88.5 213.8 %all-gather.4.cloned.1.call-start = ((), (), s32[]{:S(2)}) async-start(), calls=%async_computation.2 | async-start | bytes 7864320 | tf_op jit(solution)/shard_map/all_gather | solution.py:139
  92.7 289.5 %all-gather.8.cloned.1.call-start = ((), (), s32[]{:S(2)}) async-start(), calls=%async_computation.5 | async-start | bytes 2621440 | tf_op jit(solution)/shard_map/all_gather | solution.py:244
  94.6 70.2 %collective-permute-start = (bf16[3,384,768]{2,1,0:T(8,128)(2,1)S(1)}, bf16[3,384,768]{2,1,0:T(8,128)(2,1)S(1)}, u32[]{:S(2)}, u32[]{:S(2)}) collective-permute-start(bf16[3,384,768]{2,1,0:T(8,128)(2,1)S(1)} %dynamic-slice_bitcast_fusion), channel_id=1, source_target_pairs={{0,4},{4,8},{8,12},{1,5},{5,9},{9,13},{2,6},{6,10},{10,14},{3,7},{... | collective-permute-start | bytes 5308424 | tf_op jit(solution)/shard_map/ppermute | solution.py:154
  96.3 74.3 %collective-permute-start.1 = (bf16[3,384,768]{2,1,0:T(8,128)(2,1)S(1)}, bf16[3,384,768]{2,1,0:T(8,128)(2,1)S(1)}, u32[]{:S(2)}, u32[]{:S(2)}) collective-permute-start(bf16[3,384,768]{2,1,0:T(8,128)(2,1)S(1)} %dynamic-slice_bitcast_fusion), channel_id=1, source_target_pairs={{4,0},{8,4},{12,8},{5,1},{9,5},{13,9},{6,2},{10,6},{14,10},{7,3},{... | collective-permute-start | bytes 5308424 | tf_op jit(solution)/shard_map/ppermute | solution.py:155
  164.8 1.3 copy-start.24
  166.1 42.2 %collective-permute-start.3 = (bf16[3,384,768]{2,1,0:T(8,128)(2,1)S(1)}, bf16[3,384,768]{2,1,0:T(8,128)(2,1)S(1)}, u32[]{:S(2)}, u32[]{:S(2)}) collective-permute-start(bf16[3,384,768]{2,1,0:T(8,128)(2,1)S(1)} %collective-permute-done), channel_id=1, source_target_pairs={{0,4},{4,8},{8,12},{1,5},{5,9},{9,13},{2,6},{6,10},{10,14},{3,7},{... | collective-permute-start | bytes 5308424 | tf_op jit(solution)/shard_map/ppermute | solution.py:154
  170.6 37.7 %copy-start.25 = (bf16[3,384,768]{2,1,0:T(8,128)(2,1)}, bf16[3,384,768]{2,1,0:T(8,128)(2,1)S(1)}, u32[]{:S(2)}) copy-start(bf16[3,384,768]{2,1,0:T(8,128)(2,1)S(1)} %collective-permute-done.1) | copy-start | bytes 5308420
  170.6 43.3 %collective-permute-start.4 = (bf16[3,384,768]{2,1,0:T(8,128)(2,1)S(1)}, bf16[3,384,768]{2,1,0:T(8,128)(2,1)}, u32[]{:S(2)}, u32[]{:S(2)}) collective-permute-start(bf16[3,384,768]{2,1,0:T(8,128)(2,1)S(1)} %collective-permute-done.1), channel_id=1, source_target_pairs={{4,0},{8,4},{12,8},{5,1},{9,5},{13,9},{6,2},{10,6},{14,10},{7,3},{... | collective-permute-start | bytes 5308424 | tf_op jit(solution)/shard_map/ppermute | solution.py:155
  208.3 41.4 %copy-start.26 = (bf16[3,384,768]{2,1,0:T(8,128)(2,1)}, bf16[3,384,768]{2,1,0:T(8,128)(2,1)S(1)}, u32[]{:S(2)}) copy-start(bf16[3,384,768]{2,1,0:T(8,128)(2,1)S(1)} %collective-permute-done.3) | copy-start | bytes 5308420
  208.3 41.4 %collective-permute-start.6 = (bf16[3,384,768]{2,1,0:T(8,128)(2,1)S(1)}, bf16[3,384,768]{2,1,0:T(8,128)(2,1)}, u32[]{:S(2)}, u32[]{:S(2)}) collective-permute-start(bf16[3,384,768]{2,1,0:T(8,128)(2,1)S(1)} %collective-permute-done.3), channel_id=1, source_target_pairs={{0,4},{4,8},{8,12},{1,5},{5,9},{9,13},{2,6},{6,10},{10,14},{3,7},{... | collective-permute-start | bytes 5308424 | tf_op jit(solution)/shard_map/ppermute | solution.py:154
  213.9 41.4 %collective-permute-start.7 = (bf16[3,384,768]{2,1,0:T(8,128)(2,1)}, bf16[3,384,768]{2,1,0:T(8,128)(2,1)}, u32[]{:S(2)}, u32[]{:S(2)}) collective-permute-start(bf16[3,384,768]{2,1,0:T(8,128)(2,1)} %collective-permute-done.4), channel_id=1, source_target_pairs={{4,0},{8,4},{12,8},{5,1},{9,5},{13,9},{6,2},{10,6},{14,10},{7,3},{... | collective-permute-start | bytes 5308424 | tf_op jit(solution)/shard_map/ppermute | solution.py:155
  215.2 47.0 %copy-start.31 = (s32[4]{0:T(128)S(1)}, s32[4]{0:T(128)}, u32[]{:S(2)}) copy-start(s32[4]{0:T(128)} %param.20) | copy-start | bytes 52
  215.2 47.1 %copy-start.35 = (s32[4]{0:T(128)S(1)}, s32[4]{0:T(128)}, u32[]{:S(2)}) copy-start(s32[4]{0:T(128)} %constant.76.clone) | copy-start | bytes 52
  215.2 48.3 %copy-start.34 = (s32[4]{0:T(128)S(1)}, s32[4]{0:T(128)}, u32[]{:S(2)}) copy-start(s32[4]{0:T(128)} %constant.75.clone) | copy-start | bytes 52
  215.2 49.5 %copy-start.33 = (s32[4]{0:T(128)S(1)}, s32[4]{0:T(128)}, u32[]{:S(2)}) copy-start(s32[4]{0:T(128)} %constant.74.clone) | copy-start | bytes 52
  215.2 52.6 %copy-start.30 = (f32[3,6,128]{2,1,0:T(8,128)S(1)}, f32[3,6,128]{2,1,0:T(8,128)}, u32[]{:S(2)}) copy-start(f32[3,6,128]{2,1,0:T(8,128)} %param.30) | copy-start | bytes 27652
  215.3 53.3 %copy-start.32 = (s32[4]{0:T(128)S(1)}, s32[4]{0:T(128)}, u32[]{:S(2)}) copy-start(s32[4]{0:T(128)} %param.18) | copy-start | bytes 52
  215.3 54.4 %copy-start.22 = (bf16[4,64,1024]{2,1,0:T(8,128)(2,1)S(1)}, bf16[4,64,1024]{2,1,0:T(8,128)(2,1)}, u32[]{:S(2)}) copy-start(bf16[4,64,1024]{2,1,0:T(8,128)(2,1)} %param.17) | copy-start | bytes 1572868
  260.5 20.7 %copy-start.17 = (bf16[3,384,768]{2,1,0:T(8,128)(2,1)}, bf16[3,384,768]{2,1,0:T(8,128)(2,1)S(1)}, u32[]{:S(2)}) copy-start(bf16[3,384,768]{2,1,0:T(8,128)(2,1)S(1)} %get-tuple-element.7) | copy-start | bytes 5308420
  260.5 41.7 %collective-permute-start.8 = (bf16[3,384,768]{2,1,0:T(8,128)(2,1)S(1)}, bf16[3,384,768]{2,1,0:T(8,128)(2,1)}, u32[]{:S(2)}, u32[]{:S(2)}) collective-permute-start(bf16[3,384,768]{2,1,0:T(8,128)(2,1)S(1)} %get-tuple-element.7), channel_id=1, source_target_pairs={{16,0},{0,16},{17,1},{1,17},{18,2},{2,18},{19,3},{3,19},{20,4},{4,... | collective-permute-start | bytes 5308424 | tf_op jit(solution)/shard_map/ppermute | solution.py:174
  269.2 70.9 %collective-permute-start.5 = (bf16[3,384,768]{2,1,0:T(8,128)(2,1)}, bf16[3,384,768]{2,1,0:T(8,128)(2,1)}, u32[]{:S(2)}, u32[]{:S(2)}) collective-permute-start(bf16[3,384,768]{2,1,0:T(8,128)(2,1)} %get-tuple-element.6), channel_id=1, source_target_pairs={{16,0},{0,16},{17,1},{1,17},{18,2},{2,18},{19,3},{3,19},{20,4},{4,... | collective-permute-start | bytes 5308424 | tf_op jit(solution)/shard_map/ppermute | solution.py:174
  271.8 198.9 %reduce-scatter.5.cloned.1.call-start = ((), (), s32[]{:S(2)}) async-start(), calls=%async_computation.6 | async-start | bytes 3932160 | tf_op jit(solution)/shard_map/reduce_scatter | solution.py:256
  281.3 93.6 %collective-permute-start.2 = (bf16[3,384,768]{2,1,0:T(8,128)(2,1)}, bf16[3,384,768]{2,1,0:T(8,128)(2,1)}, u32[]{:S(2)}, u32[]{:S(2)}) collective-permute-start(bf16[3,384,768]{2,1,0:T(8,128)(2,1)} %get-tuple-element.5), channel_id=1, source_target_pairs={{16,0},{0,16},{17,1},{1,17},{18,2},{2,18},{19,3},{3,19},{20,4},{4,... | collective-permute-start | bytes 5308424 | tf_op jit(solution)/shard_map/ppermute | solution.py:174
  302.3 37.9 %copy-start.6 = (bf16[1024,3072]{1,0:T(8,128)(2,1)S(1)}, bf16[1024,3072]{1,0:T(8,128)(2,1)}, u32[]{:S(2)}) copy-start(bf16[1024,3072]{1,0:T(8,128)(2,1)} %all-gather.4.cloned.1.call-done) | copy-start | bytes 18874372
  384.5 1.9 copy-start.21
  386.4 1.9 copy-start.20
  405.3 1.5 copy-start.19
  406.7 12.1 %slice-start = ((s8[6291456]{0:T(1024)(128)(4,1)}), s8[4194304]{0:T(1024)(128)(4,1)S(1)}, s32[]{:S(2)}) async-start(s8[6291456]{0:T(1024)(128)(4,1)} %bitcast.131), calls=%async_computation.7 | async-start | bytes 8388608
  410.7 8.2 %slice-start.1 = ((s8[6291456]{0:T(1024)(128)(4,1)}), s8[2097152]{0:T(1024)(128)(4,1)S(1)}, s32[]{:S(2)}) async-start(s8[6291456]{0:T(1024)(128)(4,1)} %bitcast.131), calls=%async_computation.8 | async-start | bytes 4194304
  434.6 3.9 copy-start.27
  441.5 6.2 %copy-start.18 = (bf16[3,384,768]{2,1,0:T(8,128)(2,1)S(1)}, bf16[3,384,768]{2,1,0:T(8,128)(2,1)}, u32[]{:S(2)}) copy-start(bf16[3,384,768]{2,1,0:T(8,128)(2,1)} %copy-done.17) | copy-start | bytes 5308420
  444.6 3.1 copy-start.10
  444.6 4.1 copy-start.12
  444.6 5.0 copy-start.13
  449.6 7.4 %copy-start.8 = (f32[1024,768]{1,0:T(8,128)S(1)}, f32[1024,768]{1,0:T(8,128)}, u32[]{:S(2)}) copy-start(f32[1024,768]{1,0:T(8,128)} %fusion.54) | copy-start | bytes 9437188
  449.6 7.4 %copy-start.9 = (f32[1024,768]{1,0:T(8,128)S(1)}, f32[1024,768]{1,0:T(8,128)}, u32[]{:S(2)}) copy-start(f32[1024,768]{1,0:T(8,128)} %fusion.63) | copy-start | bytes 9437188
  449.6 7.4 %copy-start.11 = (f32[1024,768]{1,0:T(8,128)S(1)}, f32[1024,768]{1,0:T(8,128)}, u32[]{:S(2)}) copy-start(f32[1024,768]{1,0:T(8,128)} %fusion.75) | copy-start | bytes 9437188
  456.9 7.5 %copy-start.14 = (f32[1024,768]{1,0:T(8,128)S(1)}, f32[1024,768]{1,0:T(8,128)}, u32[]{:S(2)}) copy-start(f32[1024,768]{1,0:T(8,128)} %fusion.77) | copy-start | bytes 9437188
  456.9 7.5 %copy-start.15 = (f32[1024,768]{1,0:T(8,128)S(1)}, f32[1024,768]{1,0:T(8,128)}, u32[]{:S(2)}) copy-start(f32[1024,768]{1,0:T(8,128)} %fusion.56) | copy-start | bytes 9437188
  456.9 7.5 %copy-start.16 = (f32[1024,768]{1,0:T(8,128)S(1)}, f32[1024,768]{1,0:T(8,128)}, u32[]{:S(2)}) copy-start(f32[1024,768]{1,0:T(8,128)} %fusion.71) | copy-start | bytes 9437188
  470.7 1.9 copy-start.2
  472.6 1.9 copy-start.3
  474.5 1.9 copy-start.4
  476.4 1.1 copy-start.5
  477.5 17.1 %copy-start.1 = (bf16[8,4096,16]{1,2,0:T(8,128)(2,1)S(1)}, bf16[8,4096,16]{1,2,0:T(8,128)(2,1)}, u32[]{:S(2)}) copy-start(bf16[8,4096,16]{1,2,0:T(8,128)(2,1)} %param.24) | copy-start | bytes 3145732
Sparse Core Ops, SparseCore 0:
  9.8 48.6 all-gather.5
  88.6 69.9 reduce-scatter.2
  405.4 59.7 reduce-scatter.4
Sparse Core Ops, SparseCore 1:
  92.8 44.9 all-gather.3
  271.9 21.7 all-gather.7

commit v2 on v1

--- a/solution.py
+++ b/solution.py
@@ -28,17 +28,6 @@
             found += [(source, way, steps) for source, way in pair if 0 <= source < count]
         plan.append(found)
     return plan
-
-
-def chunk_product(tokens, weight):
-    return [
-        jnp.dot(tokens, weight[j], preferred_element_type=jnp.float32)
-        for j in range(weight.shape[0])
-    ]
-
-
-def added(left, right):
-    return [a + b for a, b in zip(left, right)]
 
 
 def attention_kernel(
@@ -130,55 +119,64 @@
     return (normal_rows * (1.0 + scale_row) + shift_row).astype(jnp.bfloat16)
 
 
-def image_part(image_token_activations, modulation, image_weight):
-    replicas = lax.axis_size("groups")
-    count = lax.axis_size("seq")
-    my_replica = lax.axis_index("groups")
-    place = lax.axis_index("seq")
-    modulated = modulated_rows(image_token_activations, modulation)
-    full_image = lax.all_gather(modulated, "heads", axis=0, tiled=True)
-    depth = image_weight.shape[0]
-    share = depth // replicas
-    own = image_weight.transpose(1, 0, 2)
-    piece = lax.dynamic_slice_in_dim(own, my_replica * share, share, 1)
-
-    def tokens_of(first, length):
-        return lax.dynamic_slice_in_dim(full_image, first, length, 1)
-
-    plan = line_plan(count)
-    going_up = [(i, i + 1) for i in range(count - 1)]
-    going_down = [(i + 1, i) for i in range(count - 1)]
-    up, down = [piece], [piece]
-    total = chunk_product(tokens_of(place * depth, depth), own)
-    for step in range(1, count):
-        up.append(lax.ppermute(up[-1], "seq", going_up))
-        down.append(lax.ppermute(down[-1], "seq", going_down))
+class Gather:
+    def __init__(self, weight):
+        self.replicas = lax.axis_size("groups")
+        self.count = lax.axis_size("seq")
+        self.replica = lax.axis_index("groups")
+        self.place = lax.axis_index("seq")
+        self.depth = weight.shape[0]
+        self.share = self.depth // self.replicas
+        own = weight.transpose(1, 0, 2)
+        self.whole = jnp.zeros((own.shape[0], self.depth * self.count, own.shape[2]), own.dtype)
+        self.put(own, self.place * self.depth)
+        piece = lax.dynamic_slice_in_dim(own, self.replica * self.share, self.share, 1)
+        self.up, self.down = [piece], [piece]
+        self.plan = line_plan(self.count)
+
+    def put(self, rows, first):
+        self.whole = lax.dynamic_update_slice_in_dim(self.whole, rows, first, 1)
+
+    def travel(self):
+        last = self.count - 1
+        self.up.append(lax.ppermute(self.up[-1], "seq", [(i, i + 1) for i in range(last)]))
+        self.down.append(lax.ppermute(self.down[-1], "seq", [(i + 1, i) for i in range(last)]))
+
+    def pick(self, step):
         choices = {}
-        for here in range(count):
-            source, way, steps = plan[here][step - 1]
+        for here in range(self.count):
+            source, way, steps = self.plan[here][step - 1]
             choices.setdefault((way, steps), []).append(here)
         chosen = None
         for (way, steps), places in choices.items():
-            array = (up if way == "up" else down)[steps]
+            array = (self.up if way == "up" else self.down)[steps]
             if chosen is None:
                 chosen = array
             else:
-                here = functools.reduce(jnp.logical_or, [place == i for i in places])
+                here = functools.reduce(jnp.logical_or, [self.place == i for i in places])
                 chosen = jnp.where(here, array, chosen)
-        source = jnp.array([plan[here][step - 1][0] for here in range(count)], jnp.int32)[place]
-        chosen = lax.optimization_barrier(chosen)
-        total = added(
-            total, chunk_product(tokens_of(source * depth + my_replica * share, share), chosen)
-        )
-        for turn in range(1, replicas):
-            theirs = lax.ppermute(
-                chosen, "groups", [((i + turn) % replicas, i) for i in range(replicas)]
+        sources = [self.plan[here][step - 1][0] for here in range(self.count)]
+        return chosen, jnp.array(sources, jnp.int32)[self.place] * self.depth
+
+    def swap(self, chosen):
+        return [
+            lax.ppermute(
+                chosen, "groups", [((i + turn) % self.replicas, i) for i in range(self.replicas)]
             )
-            replica = lax.rem(my_replica + turn, replicas)
-            total = added(
-                total, chunk_product(tokens_of(source * depth + replica * share, share), theirs)
-            )
-    return total
+            for turn in range(1, self.replicas)
+        ]
+
+    def keep(self, chosen, theirs, first):
+        self.put(chosen, first + self.replica * self.share)
+        for turn, rows in enumerate(theirs, 1):
+            replica = lax.rem(self.replica + turn, self.replicas)
+            self.put(rows, first + replica * self.share)
+
+
+def tied(gather, *arrays):
+    held = lax.optimization_barrier((gather.up[-1], gather.down[-1]) + arrays)
+    gather.up[-1], gather.down[-1] = held[:2]
+    return held[2:]
 
 
 def local(
@@ -200,8 +198,16 @@
     requests = prompt_token_input.shape[0]
     positions = prompt_token_input.shape[1]
     my_slot = lax.axis_index("seq")
+    steps = lax.axis_size("seq") - 1
+    gather = Gather(image_query_key_value_weight)
     whole = lax.all_gather(prompt_token_input, "seq", axis=2, tiled=True)
-    image_proj = image_part(image_token_activations, modulation, image_query_key_value_weight)
+    modulated = modulated_rows(image_token_activations, modulation)
+    text_weight = text_key_value_weight.reshape(text_key_value_weight.shape[0], -1)
+    whole, modulated, text_weight = tied(gather, whole, modulated, text_weight)
+
+    full_image = lax.all_gather(modulated, "heads", axis=0, tiled=True)
+    for _ in range(steps - 2):
+        gather.travel()
     width = whole.shape[2]
     normed = rms_rows(whole.astype(jnp.float32)).astype(jnp.bfloat16)
     tenant_adapters = adapter_down_maps.shape[0]
@@ -237,23 +243,53 @@
     partial = jnp.einsum(
         "rpf,fd->rpd", hidden, encoder_down_weight, preferred_element_type=jnp.float32
     ).astype(jnp.bfloat16)
+    partial, full_image = tied(gather, partial, full_image)
+
     summed = lax.psum_scatter(partial, "seq", scatter_dimension=2, tiled=True)
+    gather.travel()
+    waiting = []
+    for step in range(1, steps - 1):
+        chosen, first = gather.pick(step)
+        waiting.append((chosen, gather.swap(chosen), first))
     encoded = (
         summed.astype(jnp.float32) + prompt_token_input.astype(jnp.float32)
     ).astype(jnp.bfloat16)
+    (encoded,) = tied(gather, encoded)
+
     prompts = lax.all_gather(encoded, "heads", axis=1, tiled=True)
+    gather.travel()
+    chosen, first = gather.pick(steps - 1)
+    waiting.append((chosen, gather.swap(chosen), first))
+    for chosen, theirs, first in waiting:
+        gather.keep(chosen, theirs, first)
     text_count = prompts.shape[1]
     ordered = jnp.take(prompts, prompt_order, axis=0).reshape(requests * text_count, -1)
-    text_partial = jnp.concatenate(
-        [
-            jnp.dot(
-                ordered, text_key_value_weight[:, j], preferred_element_type=jnp.float32
-            ).astype(jnp.bfloat16)
-            for j in range(2)
-        ],
-        axis=1,
-    ).reshape(requests, text_count, -1)
+    text_partial = (
+        jnp.dot(ordered, text_weight, preferred_element_type=jnp.float32)
+        .astype(jnp.bfloat16)
+        .reshape(requests, text_count, -1)
+    )
+    text_partial, gather.whole = tied(gather, text_partial, gather.whole)
+
     text = lax.psum_scatter(text_partial, "seq", scatter_dimension=0, tiled=True)[0]
+    chosen, first = gather.pick(steps)
+    theirs = gather.swap(chosen)
+    gather.keep(chosen, [], first)
+    image_proj = [
+        jnp.dot(full_image, gather.whole[j], preferred_element_type=jnp.float32)
+        for j in range(gather.whole.shape[0])
+    ]
+    *theirs, held = lax.optimization_barrier((*theirs, tuple(image_proj)))
+    for turn, rows in enumerate(theirs, 1):
+        replica = lax.rem(gather.replica + turn, gather.replicas)
+        tokens = lax.dynamic_slice_in_dim(
+            full_image, first + replica * gather.share, gather.share, 1
+        )
+        held = [
+            total + jnp.dot(tokens, rows[j], preferred_element_type=jnp.float32)
+            for j, total in enumerate(held)
+        ]
+    image_proj = held
     output = attention(
         live_length, query_key_norm_gain, image_proj[0], image_proj[1], image_proj[2], text
     )

time: 507 us -> 337 us (0.66)
  waiting for transfers between devices: 267 us -> 157 us
  matrix products: 121 us -> 65.9 us
  other arithmetic: 14.6 us -> 25.4 us
  local copies, waits for them, and re-layouts: 43.9 us -> 35.7 us
    ppermute x9, waiting for transfers between devices: 220 us -> 57.9 us  [the longest x3 48.2 us: swap(): lax.ppermute(chosen, 'groups', [((i + turn) % self.replicas, i) for i in...]
    reduce_scatter x1, waiting for transfers between devices: 0.01 us -> 55.4 us  [local(): summed = lax.psum_scatter(partial, 'seq', scatter_dimension=2, tiled=True)]
    dot_general x23 -> x7, matrix products: 88.6 us -> 34.5 us  [the longest x3 23.3 us: local(): jnp.dot(full_image, gather.whole[j], preferred_element_type=jnp.float32)]
    concatenate x1 -> x0, local copies, waits for them, and re-layouts: 13.1 us -> none  [local(): jnp.concatenate([jnp.dot(ordered, text_key_value_weight[:, j], preferred_...]
    dynamic_update_slice x0 -> x3, other arithmetic: none -> 11.5 us  [put(): self.whole = lax.dynamic_update_slice_in_dim(self.whole, rows, first, 1)]
    slice x1 -> x0, local copies, waits for them, and re-layouts: 9.44 us -> none  [local(): text_key_value_weight[:, j]]
    dynamic_update_slice x0 -> x3, local copies, waits for them, and re-layouts: none -> 8.24 us  [put(): self.whole = lax.dynamic_update_slice_in_dim(self.whole, rows, first, 1)]
    add x0 -> x3, other arithmetic: none -> 6.2 us  [local(): total + jnp.dot(tokens, rows[j], preferred_element_type=jnp.float32)]
  transfers between devices with their start and end apart: 14 -> 14, of which waited for: 8 -> 9; matrix products, arithmetic and copies ran while one was open for 23% -> 35% of each run, Pallas kernels for 0% -> 0%
where the time goes in v2:
time: 337 us; the launch traced here: 336 us
  waiting for transfers between devices  157 us (47%)
  matrix products  65.9 us (20%)
  local copies, waits for them, and re-layouts  35.7 us (11%)
  other arithmetic  25.4 us (8%)
  starting transfers between devices  17.9 us (5%)
  between operations  17.4 us (5%)
  Pallas kernels  17.1 us (5%)
    reduce_scatter x1, waiting for transfers between devices, local(): summed = lax.psum_scatter(partial, 'seq', scatter_dimension=2, tiled=True)  55.4 us
    ppermute x3, waiting for transfers between devices, swap(): lax.ppermute(chosen, 'groups', [((i + turn) % self.replicas, i) for i in...  48.2 us
    all_gather x1, waiting for transfers between devices, local(): whole = lax.all_gather(prompt_token_input, 'seq', axis=2, tiled=True)  40.3 us
    dot_general x3, matrix products, local(): jnp.dot(full_image, gather.whole[j], preferred_element_type=jnp.float32)  23.3 us
    pallas_call x1, Pallas kernels, attention(): pl.pallas_call(functools.partial(attention_kernel, rows_per_step=rows_per...  17.1 us
    dot_general x1, matrix products, local(): jnp.einsum('rpf,fd->rpd', hidden, encoder_down_weight, preferred_element_...  16.2 us
    unnamed x42, local copies, waits for them, and re-layouts  13.1 us
    dynamic_update_slice x3, other arithmetic, put(): self.whole = lax.dynamic_update_slice_in_dim(self.whole, rows, first, 1)  11.5 us
  transfers between devices with their start and end apart: 14, of which 9 were waited for; matrix products, arithmetic and copies ran while one was open for 35% of the time, Pallas kernels for 0%

profile of v2, /device:TPU:0, one launch (start us, length us, event | category | flops | bytes accessed | tf_op | source)
XLA Modules:
  0.0 336.5 jit_solution(16951500850719071724)
XLA Ops:
  6.5 0.7 all-gather.4.cloned.1.call-update
  7.3 4.1 %copy.24 = bf16[128,8,2,768]{3,1,2,0:T(8,128)(2,1)} copy(bf16[128,8,2,768]{3,2,1,0:T(2,128)(2,1)} %bitcast.87) | data formatting | bytes 6291456
  11.5 2.9 dynamic-slice_bitcast_fusion
  14.4 0.3 convert_reduce_fusion
  14.7 0.6 fusion.17
  15.3 1.9 fusion.20
  17.3 40.3 %all-gather.4.cloned.1.call-done = bf16[4,64,4096]{2,1,0:T(8,128)(2,1)} async-done(((bf16[4,64,1024]{2,1,0:T(8,128)(2,1)}), bf16[4,64,4096]{2,1,0:T(8,128)(2,1)}) %all-gather.4.cloned.1.call-update) | async-done | bytes 2097168 | tf_op jit(solution)/shard_map/all_gather | solution.py:203
  57.7 0.3 fusion.62
  58.0 1.3 fusion.46
  59.3 1.9 collective-permute-start
  61.2 1.5 collective-permute-start.1
  62.7 2.3 fusion.12
  65.0 9.4 %fusion.4 = f32[4,64,1280]{2,1,0:T(8,128)} fusion(bf16[4096,1280]{1,0:T(8,128)(2,1)} %param.21, bf16[4,64,4096]{2,1,0:T(8,128)(2,1)S(1)} %copy-done.10, f32[4,64]{1,0:T(4,128)S(1)} %add_rsqrt_fusion), kind=kOutput, calls=%fused_computation.5 | convolution fusion | flops 2687500288 | bytes 13894656 | tf_op jit(solution)/shard_map/dot_general | solution.py:227
  74.4 4.3 %fusion.42 = f32[4,64,1280]{2,1,0:T(8,128)} fusion(f32[4,64,1280]{2,1,0:T(8,128)} %fusion.4, bf16[4,64,4096]{2,1,0:T(8,128)(2,1)} %all-gather.4.cloned.1.call-done, f32[4,64]{1,0:T(4,128)S(1)} %add_rsqrt_fusion, bf16[4,4096,16]{1,0,2:T(4,128)(2,1)S(1)} %fusion.46, bf16[4,16,1280]{2,0,1:T(4,128)(2,1)S(1)} %fusion.62), kind=kOutput, calls=%fused_computation.46 | convolution fusion | flops 50466816 | bytes 5407744 | tf_op jit(solution)/shard_map/sqt,sti->sqi/dot_general | solution.py:230
  78.7 16.2 %fusion.6 = bf16[4,64,4096]{2,1,0:T(8,128)(2,1)} fusion(bf16[1280,4096]{1,0:T(8,128)(2,1)} %param.23, f32[4,64,1280]{2,1,0:T(8,128)} %fusion.42, bf16[4096,1280]{1,0:T(8,128)(2,1)} %param.22, bf16[4,64,4096]{2,1,0:T(8,128)(2,1)} %all-gather.4.cloned.1.call-done, f32[4,64]{1,0:T(4,128)S(1)} %add_rsqrt_fusion), kind=kOutput, calls=%fused_computation.9 | convolution fusion | flops 5373558784 | bytes 26477568 | tf_op jit(solution)/shard_map/rpf,fd->rpd/dot_general | solution.py:243
  94.8 4.2 %collective-permute-done = bf16[3,384,768]{2,1,0:T(8,128)(2,1)S(1)} collective-permute-done((bf16[3,384,768]{2,1,0:T(8,128)(2,1)}, bf16[3,384,768]{2,1,0:T(8,128)(2,1)S(1)}, u32[]{:S(2)}, u32[]{:S(2)}) %collective-permute-start) | collective-permute-done | bytes 1769504 | tf_op jit(solution)/shard_map/ppermute | solution.py:142
  99.0 4.4 %collective-permute-done.1 = bf16[3,384,768]{2,1,0:T(8,128)(2,1)} collective-permute-done((bf16[3,384,768]{2,1,0:T(8,128)(2,1)}, bf16[3,384,768]{2,1,0:T(8,128)(2,1)}, u32[]{:S(2)}, u32[]{:S(2)}) %collective-permute-start.1) | collective-permute-done | bytes 1769504 | tf_op jit(solution)/shard_map/ppermute | solution.py:143
  103.4 0.9 all-gather.6.cloned.1.call-done
  104.4 4.6 %collective-permute-start.2 = (bf16[3,384,768]{2,1,0:T(8,128)(2,1)S(1)}, bf16[3,384,768]{2,1,0:T(8,128)(2,1)}, u32[]{:S(2)}, u32[]{:S(2)}) collective-permute-start(bf16[3,384,768]{2,1,0:T(8,128)(2,1)S(1)} %collective-permute-done), channel_id=1, source_target_pairs={{0,4},{4,8},{8,12},{1,5},{5,9},{9,13},{2,6},{6,10},{10,14},{3,7},{... | collective-permute-start | bytes 5308424 | tf_op jit(solution)/shard_map/ppermute | solution.py:142
  109.0 1.3 collective-permute-start.3
  110.3 6.0 %broadcast_in_dim.34 = bf16[3,3072,768]{2,1,0:T(8,128)(2,1)} broadcast(bf16[]{:T(256)} %constant.71.clone.1), dimensions={} | broadcast | bytes 14155778 | tf_op jit(solution)/shard_map/broadcast_in_dim | solution.py:131
  116.3 4.1 %bitcast_dynamic-update-slice_fusion = bf16[3,3072,768]{2,1,0:T(8,128)(2,1)} fusion(bf16[3,3072,768]{2,1,0:T(8,128)(2,1)} %broadcast_in_dim.34, s32[]{:T(128)S(6)} %select_n.99, bf16[768,3,768]{2,0,1:T(8,128)(2,1)} %param.29), kind=kLoop, calls=%fused_computation.21 | loop fusion | bytes 7077892 | tf_op jit(solution)/shard_map/dynamic_update_slice | solution.py:138
  120.4 0.6 dynamic_slice.24
  121.6 3.8 %constant_dynamic-update-slice_fusion.4 = (bf16[3,3072,768]{2,1,0:T(8,128)(2,1)}, bf16[3,384,768]{2,1,0:T(8,128)(2,1)}) fusion(bf16[3,3072,768]{2,1,0:T(8,128)(2,1)} %bitcast_dynamic-update-slice_fusion, s32[]{:T(128)S(6)} %select_n.102, bf16[3,384,768]{2,1,0:T(8,128)(2,1)S(1)} %collective-permute-done, bf16[3,384,768]{2,1,0:T(8,128)(2,1)} %collective-permute-done.1, ...), kind=kLoop, calls=%fused_computation.83 | loop fusion | flops 884736 | bytes 7077893 | tf_op jit(solution)/shard_map/dynamic_update_slice | solution.py:138
  125.4 1.4 collective-permute-start.6
  126.8 55.4 %reduce-scatter.3.cloned.1.call-done = bf16[4,64,1024]{2,1,0:T(8,128)(2,1)} async-done(((bf16[4,64,4096]{2,1,0:T(8,128)(2,1)}), bf16[4,64,1024]{2,1,0:T(8,128)(2,1)}) %reduce-scatter.3.cloned.1.call-update) | async-done | bytes 524304 | tf_op jit(solution)/shard_map/reduce_scatter | solution.py:248
  182.2 2.0 add_convert_fusion
  184.2 1.1 collective-permute-done.3
  185.4 0.3 reduce-scatter.5.cloned.1.call-start
  185.7 0.6 dynamic_slice.25
  187.0 2.8 constant_dynamic-update-slice_fusion.3
  189.8 4.2 %constant_dynamic-update-slice_fusion.2 = (bf16[3,3072,768]{2,1,0:T(8,128)(2,1)}, bf16[3,384,768]{2,1,0:T(8,128)(2,1)}) fusion(bf16[3,3072,768]{2,1,0:T(8,128)(2,1)} %constant_dynamic-update-slice_fusion.3, s32[]{:T(128)S(6)} %select_n.109, bf16[3,384,768]{2,1,0:T(8,128)(2,1)} %collective-permute-done.2, bf16[3,384,768]{2,1,0:T(8,128)(2,1)} %collective-permute-done.1, ...), kind=kLoop, calls=%fused_computation.81 | loop fusion | flops 2654208 | bytes 10616839 | tf_op jit(solution)/shard_map/dynamic_update_slice | solution.py:138
  194.0 1.5 collective-permute-start.7
  195.5 0.1 select_reduce_fusion
  195.6 2.5 collective-permute-start.4
  198.1 1.3 collective-permute-start.5
  199.5 34.3 %collective-permute-done.7 = bf16[3,384,768]{2,1,0:T(8,128)(2,1)S(1)} collective-permute-done((bf16[3,384,768]{2,1,0:T(8,128)(2,1)}, bf16[3,384,768]{2,1,0:T(8,128)(2,1)S(1)}, u32[]{:S(2)}, u32[]{:S(2)}) %collective-permute-start.7) | collective-permute-done | bytes 1769504 | tf_op jit(solution)/shard_map/ppermute | solution.py:163
  233.9 1.3 constant_dynamic-update-slice_fusion.1
  235.2 2.3 gather_fusion
  237.5 0.4 bitcast_select_fusion
  237.9 1.5 copy-done.8
  239.4 4.8 %convolution_convert_fusion = bf16[1024,1536]{1,0:T(8,128)(2,1)} fusion(bf16[1024,1024]{1,0:T(8,128)(2,1)S(1)} %bitcast_select_fusion, bf16[1024,1536]{1,0:T(8,128)(2,1)S(1)} %bitcast.88), kind=kOutput, calls=%fused_computation.20 | convolution fusion | flops 3222798336 | bytes 8388608 | tf_op jit(solution)/shard_map/dot_general | solution.py:268
  244.2 0.6 copy-done.17
  244.8 0.6 dynamic_slice.26
  246.1 0.6 dynamic_slice.21
  248.7 0.7 dynamic_slice.22.live_ref
  249.3 3.6 %constant_dynamic-update-slice_fusion = (bf16[3,3072,768]{2,1,0:T(8,128)(2,1)}, bf16[3,384,768]{2,1,0:T(8,128)(2,1)S(1)}) fusion(bf16[3,3072,768]{2,1,0:T(8,128)(2,1)} %constant_dynamic-update-slice_fusion.1, s32[]{:T(128)S(6)} %select_n.114, bf16[3,384,768]{2,1,0:T(8,128)(2,1)} %collective-permute-done.4, bf16[3,384,768]{2,1,0:T(8,128)(2,1)} %collective-permute-done.2, ...), kind=kLoop, calls=%fused_computation.79 | loop fusion | flops 2654208 | bytes 10616839 | tf_op jit(solution)/shard_map/dynamic_update_slice | solution.py:138
  252.9 1.5 collective-permute-start.8
  254.4 8.7 %fusion.9 = f32[1024,768]{1,0:T(8,128)S(1)} fusion(bf16[1024,3072]{1,0:T(8,128)(2,1)} %all-gather.6.cloned.1.call-done, bf16[3,3072,768]{2,1,0:T(8,128)(2,1)} %get-tuple-element.45), kind=kOutput, calls=%fused_computation.11 | convolution fusion | flops 4831838208 | bytes 14155776 | tf_op jit(solution)/shard_map/dot_general | solution.py:279
  263.1 7.2 %fusion.10 = f32[1024,768]{1,0:T(8,128)S(1)} fusion(bf16[1024,3072]{1,0:T(8,128)(2,1)} %all-gather.6.cloned.1.call-done, bf16[3,3072,768]{2,1,0:T(8,128)(2,1)S(1)} %copy-done.7), kind=kOutput, calls=%fused_computation.13 | convolution fusion | flops 4831838208 | bytes 14155776 | tf_op jit(solution)/shard_map/dot_general | solution.py:279
  270.3 7.4 %fusion.11 = f32[1024,768]{1,0:T(8,128)S(1)} fusion(bf16[1024,3072]{1,0:T(8,128)(2,1)} %all-gather.6.cloned.1.call-done, bf16[3,3072,768]{2,1,0:T(8,128)(2,1)S(1)} %copy-done.7), kind=kOutput, calls=%fused_computation.15 | convolution fusion | flops 4831838208 | bytes 14155776 | tf_op jit(solution)/shard_map/dot_general | solution.py:279
  277.8 13.9 %collective-permute-done.8 = bf16[3,384,768]{2,1,0:T(8,128)(2,1)S(1)} collective-permute-done((bf16[3,384,768]{2,1,0:T(8,128)(2,1)S(1)}, bf16[3,384,768]{2,1,0:T(8,128)(2,1)S(1)}, u32[]{:S(2)}, u32[]{:S(2)}) %collective-permute-start.8) | collective-permute-done | bytes 1769504 | tf_op jit(solution)/shard_map/ppermute | solution.py:163
  291.7 2.1 fusion.50
  293.8 2.1 add.177.value_ref
  295.9 2.1 fusion.52
  298.0 2.0 add.176.key_ref
  300.0 2.1 fusion.54
  302.2 2.1 add.175.query_ref
  304.3 1.8 reduce-scatter.5.cloned.1.call-done
  306.1 1.9 copy-done.2
  307.9 1.9 copy-done.3
  309.8 1.9 copy-done.4
  311.7 1.1 copy-done.5
  312.9 17.1 %shard_map.163 = bf16[1024,768]{1,0:T(8,128)(2,1)} custom-call(s32[1]{0:T(128)} %dynamic_slice.22.live_ref, f32[6,3,128]{2,1,0:T(4,128)S(1)} %bitcast.84, f32[1024,768]{1,0:T(8,128)S(1)} %copy-done.4, f32[1024,768]{1,0:T(8,128)S(1)} %copy-done.3, f32[1024,768]{1,0:T(8,128)S(1)} %copy-done.2, bf16[256,1536]{1,0:T(8,128)(2,1)S(1)} %bitcast.85, ...), custom_call_target="tpu_custom_call" | custom-call | flops 4026531840 | bytes 11796480 | tf_op jit(solution)/shard_map/pallas_call | solution.py:87
  (58 shorter events, 0.4 us)
Async XLA Ops:
  6.5 51.5 %copy-start = (bf16[8,4096,16]{1,2,0:T(8,128)(2,1)S(1)}, bf16[8,4096,16]{1,2,0:T(8,128)(2,1)}, u32[]{:S(2)}) copy-start(bf16[8,4096,16]{1,2,0:T(8,128)(2,1)} %param.24) | copy-start | bytes 3145732
  6.5 51.1 %all-gather.4.cloned.1.call-start = ((), (), s32[]{:S(2)}) async-start(), calls=%async_computation.2 | async-start | bytes 2621440 | tf_op jit(solution)/shard_map/all_gather | solution.py:203
  7.3 97.0 %all-gather.6.cloned.1.call-start = ((), (), s32[]{:S(2)}) async-start(), calls=%async_computation.3 | async-start | bytes 7864320 | tf_op jit(solution)/shard_map/all_gather | solution.py:208
  11.5 2.9 copy-start.6
  11.5 3.8 %copy-start.12 = (bf16[1,2,3072]{2,1,0:T(2,128)(2,1)S(1)}, bf16[1,2,3072]{2,1,0:T(2,128)(2,1)}, u32[]{:S(2)}) copy-start(bf16[1,2,3072]{2,1,0:T(2,128)(2,1)} %param.28) | copy-start | bytes 36868
  14.7 43.0 %copy-start.11 = (bf16[8,16,1280]{2,1,0:T(8,128)(2,1)S(1)}, bf16[8,16,1280]{2,1,0:T(8,128)(2,1)}, u32[]{:S(2)}) copy-start(bf16[8,16,1280]{2,1,0:T(8,128)(2,1)} %param.25) | copy-start | bytes 983044
  14.7 43.0 %copy-start.14 = (s32[4]{0:T(128)S(1)}, s32[4]{0:T(128)}, u32[]{:S(2)}) copy-start(s32[4]{0:T(128)} %param.19) | copy-start | bytes 52
  57.6 124.6 %reduce-scatter.3.cloned.1.call-start = ((), (), s32[]{:S(2)}) async-start(), calls=%async_computation.4 | async-start | bytes 2621440 | tf_op jit(solution)/shard_map/reduce_scatter | solution.py:248
  57.7 7.3 %copy-start.10 = (bf16[4,64,4096]{2,1,0:T(8,128)(2,1)S(1)}, bf16[4,64,4096]{2,1,0:T(8,128)(2,1)}, u32[]{:S(2)}) copy-start(bf16[4,64,4096]{2,1,0:T(8,128)(2,1)} %all-gather.4.cloned.1.call-done) | copy-start | bytes 6291460
  59.3 39.7 %collective-permute-start = (bf16[3,384,768]{2,1,0:T(8,128)(2,1)}, bf16[3,384,768]{2,1,0:T(8,128)(2,1)S(1)}, u32[]{:S(2)}, u32[]{:S(2)}) collective-permute-start(bf16[3,384,768]{2,1,0:T(8,128)(2,1)} %dynamic-slice_bitcast_fusion), channel_id=1, source_target_pairs={{0,4},{4,8},{8,12},{1,5},{5,9},{9,13},{2,6},{6,10},{10,14},{3,7},{... | collective-permute-start | bytes 5308424 | tf_op jit(solution)/shard_map/ppermute | solution.py:142
  61.2 42.2 %collective-permute-start.1 = (bf16[3,384,768]{2,1,0:T(8,128)(2,1)}, bf16[3,384,768]{2,1,0:T(8,128)(2,1)}, u32[]{:S(2)}, u32[]{:S(2)}) collective-permute-start(bf16[3,384,768]{2,1,0:T(8,128)(2,1)} %dynamic-slice_bitcast_fusion), channel_id=1, source_target_pairs={{4,0},{8,4},{12,8},{5,1},{9,5},{13,9},{6,2},{10,6},{14,10},{7,3},{... | collective-permute-start | bytes 5308424 | tf_op jit(solution)/shard_map/ppermute | solution.py:143
  104.3 130.9 %all-gather.8.cloned.1.call-start = ((), (), s32[]{:S(2)}) async-start(), calls=%async_computation.5 | async-start | bytes 2621440 | tf_op jit(solution)/shard_map/all_gather | solution.py:259
  104.4 79.9 %collective-permute-start.2 = (bf16[3,384,768]{2,1,0:T(8,128)(2,1)S(1)}, bf16[3,384,768]{2,1,0:T(8,128)(2,1)}, u32[]{:S(2)}, u32[]{:S(2)}) collective-permute-start(bf16[3,384,768]{2,1,0:T(8,128)(2,1)S(1)} %collective-permute-done), channel_id=1, source_target_pairs={{0,4},{4,8},{8,12},{1,5},{5,9},{9,13},{2,6},{6,10},{10,14},{3,7},{... | collective-permute-start | bytes 5308424 | tf_op jit(solution)/shard_map/ppermute | solution.py:142
  109.0 76.4 %collective-permute-start.3 = (bf16[3,384,768]{2,1,0:T(8,128)(2,1)}, bf16[3,384,768]{2,1,0:T(8,128)(2,1)}, u32[]{:S(2)}, u32[]{:S(2)}) collective-permute-start(bf16[3,384,768]{2,1,0:T(8,128)(2,1)} %collective-permute-done.1), channel_id=1, source_target_pairs={{4,0},{8,4},{12,8},{5,1},{9,5},{13,9},{6,2},{10,6},{14,10},{7,3},{... | collective-permute-start | bytes 5308424 | tf_op jit(solution)/shard_map/ppermute | solution.py:143
  116.3 4.1 %copy-start.19 = (s32[4]{0:T(128)S(1)}, s32[4]{0:T(128)}, u32[]{:S(2)}) copy-start(s32[4]{0:T(128)} %constant.76.clone) | copy-start | bytes 52
  121.6 60.6 %copy-start.9 = (bf16[4,64,1024]{2,1,0:T(8,128)(2,1)S(1)}, bf16[4,64,1024]{2,1,0:T(8,128)(2,1)}, u32[]{:S(2)}) copy-start(bf16[4,64,1024]{2,1,0:T(8,128)(2,1)} %param.17) | copy-start | bytes 1572868
  121.6 64.1 %copy-start.18 = (s32[4]{0:T(128)S(1)}, s32[4]{0:T(128)}, u32[]{:S(2)}) copy-start(s32[4]{0:T(128)} %constant.77.clone) | copy-start | bytes 52
  125.4 61.6 %collective-permute-start.6 = (bf16[3,384,768]{2,1,0:T(8,128)(2,1)}, bf16[3,384,768]{2,1,0:T(8,128)(2,1)}, u32[]{:S(2)}, u32[]{:S(2)}) collective-permute-start(bf16[3,384,768]{2,1,0:T(8,128)(2,1)} %get-tuple-element.50), channel_id=1, source_target_pairs={{16,0},{0,16},{17,1},{1,17},{18,2},{2,18},{19,3},{3,19},{20,4},{4,... | collective-permute-start | bytes 5308424 | tf_op jit(solution)/shard_map/ppermute | solution.py:163
  185.4 120.6 %reduce-scatter.5.cloned.1.call-start = ((), (), s32[]{:S(2)}) async-start(), calls=%async_computation.6 | async-start | bytes 3932160 | tf_op jit(solution)/shard_map/reduce_scatter | solution.py:274
  189.8 5.7 %copy-start.15 = (s32[4]{0:T(128)S(1)}, s32[4]{0:T(128)}, u32[]{:S(2)}) copy-start(s32[4]{0:T(128)} %param.20) | copy-start | bytes 52
  194.0 39.9 %collective-permute-start.7 = (bf16[3,384,768]{2,1,0:T(8,128)(2,1)}, bf16[3,384,768]{2,1,0:T(8,128)(2,1)S(1)}, u32[]{:S(2)}, u32[]{:S(2)}) collective-permute-start(bf16[3,384,768]{2,1,0:T(8,128)(2,1)} %get-tuple-element.48), channel_id=1, source_target_pairs={{16,0},{0,16},{17,1},{1,17},{18,2},{2,18},{19,3},{3,19},{20,4},{4,... | collective-permute-start | bytes 5308424 | tf_op jit(solution)/shard_map/ppermute | solution.py:163
  195.6 48.6 %collective-permute-start.4 = (bf16[3,384,768]{2,1,0:T(8,128)(2,1)}, bf16[3,384,768]{2,1,0:T(8,128)(2,1)}, u32[]{:S(2)}, u32[]{:S(2)}) collective-permute-start(bf16[3,384,768]{2,1,0:T(8,128)(2,1)} %collective-permute-done.2), channel_id=1, source_target_pairs={{0,4},{4,8},{8,12},{1,5},{5,9},{9,13},{2,6},{6,10},{10,14},{3,7},{... | collective-permute-start | bytes 5308424 | tf_op jit(solution)/shard_map/ppermute | solution.py:142
  198.1 46.1 %collective-permute-start.5 = (bf16[3,384,768]{2,1,0:T(8,128)(2,1)}, bf16[3,384,768]{2,1,0:T(8,128)(2,1)}, u32[]{:S(2)}, u32[]{:S(2)}) collective-permute-start(bf16[3,384,768]{2,1,0:T(8,128)(2,1)} %collective-permute-done.3), channel_id=1, source_target_pairs={{4,0},{8,4},{12,8},{5,1},{9,5},{13,9},{6,2},{10,6},{14,10},{7,3},{... | collective-permute-start | bytes 5308424 | tf_op jit(solution)/shard_map/ppermute | solution.py:143
  237.5 1.9 copy-start.8
  244.2 0.7 copy-start.17
  244.2 3.8 %copy-start.13 = (f32[3,6,128]{2,1,0:T(8,128)S(1)}, f32[3,6,128]{2,1,0:T(8,128)}, u32[]{:S(2)}) copy-start(f32[3,6,128]{2,1,0:T(8,128)} %param.30) | copy-start | bytes 27652
  244.2 4.5 %copy-start.16 = (s32[4]{0:T(128)S(1)}, s32[4]{0:T(128)}, u32[]{:S(2)}) copy-start(s32[4]{0:T(128)} %param.18) | copy-start | bytes 52
  252.9 38.8 %collective-permute-start.8 = (bf16[3,384,768]{2,1,0:T(8,128)(2,1)S(1)}, bf16[3,384,768]{2,1,0:T(8,128)(2,1)S(1)}, u32[]{:S(2)}, u32[]{:S(2)}) collective-permute-start(bf16[3,384,768]{2,1,0:T(8,128)(2,1)S(1)} %get-tuple-element.46), channel_id=1, source_target_pairs={{16,0},{0,16},{17,1},{1,17},{18,2},{2,18},{19,3},{3,19},{20,4},{4,... | collective-permute-start | bytes 5308424 | tf_op jit(solution)/shard_map/ppermute | solution.py:163
  254.4 8.7 %copy-start.7 = (bf16[3,3072,768]{2,1,0:T(8,128)(2,1)S(1)}, bf16[3,3072,768]{2,1,0:T(8,128)(2,1)}, u32[]{:S(2)}) copy-start(bf16[3,3072,768]{2,1,0:T(8,128)(2,1)} %get-tuple-element.45) | copy-start | bytes 42467332
  306.1 1.9 copy-start.2
  307.9 1.9 copy-start.3
  309.8 1.9 copy-start.4
  311.7 1.1 copy-start.5
  312.9 17.1 %copy-start.1 = (bf16[8,4096,16]{1,2,0:T(8,128)(2,1)S(1)}, bf16[8,4096,16]{1,2,0:T(8,128)(2,1)}, u32[]{:S(2)}) copy-start(bf16[8,4096,16]{1,2,0:T(8,128)(2,1)} %param.24) | copy-start | bytes 3145732
Sparse Core Ops, SparseCore 0:
  8.9 48.6 all-gather.3
  59.2 45.0 all-gather.5
  106.6 75.5 reduce-scatter.2
  185.5 22.4 all-gather.7
  244.3 61.6 reduce-scatter.4

commit v3 on v2

--- a/solution.py
+++ b/solution.py
@@ -196,80 +196,99 @@
     query_key_norm_gain,
 ):
     requests = prompt_token_input.shape[0]
-    positions = prompt_token_input.shape[1]
+    steps = lax.axis_size("seq") - 1
     my_slot = lax.axis_index("seq")
-    steps = lax.axis_size("seq") - 1
     gather = Gather(image_query_key_value_weight)
-    whole = lax.all_gather(prompt_token_input, "seq", axis=2, tiled=True)
+    gathered = lax.all_gather(prompt_token_input, "heads", axis=1, tiled=True)
+    positions = gathered.shape[1]
+    room = requests * positions // 2
+    ends = jnp.cumsum(lengths)
+    starts = ends - lengths
+    mine = room // lax.axis_size("heads")
+    packed = lax.axis_index("heads") * mine + jnp.arange(mine, dtype=jnp.int32)
+    request = jnp.minimum(
+        jnp.sum((ends[None, :] <= packed[:, None]).astype(jnp.int32), axis=1), requests - 1
+    )
+    is_request = request[:, None] == jnp.arange(requests, dtype=jnp.int32)[None, :]
+
+    def of_request(values):
+        return jnp.sum(jnp.where(is_request, values[None, :], 0), axis=1)
+
+    position = jnp.clip(packed - of_request(starts), 0, positions - 1)
+    adapter = of_request(request_adapter_index)
+    tokens_in = jnp.take(
+        gathered.reshape(requests * positions, -1),
+        request * positions + position,
+        axis=0,
+        mode="clip",
+    )
     modulated = modulated_rows(image_token_activations, modulation)
     text_weight = text_key_value_weight.reshape(text_key_value_weight.shape[0], -1)
-    whole, modulated, text_weight = tied(gather, whole, modulated, text_weight)
-
-    full_image = lax.all_gather(modulated, "heads", axis=0, tiled=True)
     for _ in range(steps - 2):
         gather.travel()
-    width = whole.shape[2]
+    tokens_in, modulated, text_weight = tied(gather, tokens_in, modulated, text_weight)
+
+    whole = lax.all_gather(tokens_in, "seq", axis=1, tiled=True)
+    whole, modulated = tied(gather, whole, modulated)
+
+    full_image = lax.all_gather(modulated, "heads", axis=0, tiled=True)
+    waiting = []
+    for step in range(1, steps - 1):
+        chosen, first = gather.pick(step)
+        waiting.append([chosen, gather.swap(chosen), first])
+    gather.travel()
     normed = rms_rows(whole.astype(jnp.float32)).astype(jnp.bfloat16)
-    tenant_adapters = adapter_down_maps.shape[0]
-    selected_adapter = (
-        request_adapter_index[:, None] == jnp.arange(tenant_adapters, dtype=jnp.int32)[None, :]
+    tenant_adapters, width, rank = adapter_down_maps.shape
+    low_rank = lax.dot_general(
+        normed,
+        adapter_down_maps.transpose(0, 2, 1).reshape(tenant_adapters * rank, width),
+        (((1,), (1,)), ((), ())),
+        preferred_element_type=jnp.float32,
     ).astype(jnp.bfloat16)
-    selected_down_maps = jnp.einsum(
-        "mn,nhi->mhi", selected_adapter, adapter_down_maps, preferred_element_type=jnp.float32
-    ).astype(jnp.bfloat16)
-    selected_up_maps = jnp.einsum(
-        "zl,log->zog", selected_adapter, adapter_up_maps, preferred_element_type=jnp.float32
-    ).astype(jnp.bfloat16)
-    adapter_projected = jnp.einsum(
-        "rpd,rdk->rpk", normed, selected_down_maps, preferred_element_type=jnp.float32
-    ).astype(jnp.bfloat16)
-    flattened = normed.reshape(requests * positions, width)
-    gated_hidden = jnp.dot(
-        flattened, encoder_gate_weight, preferred_element_type=jnp.float32
-    ).reshape(requests, positions, -1)
-    gated_hidden = gated_hidden + adapter_scale * jnp.einsum(
-        "sqt,sti->sqi", adapter_projected, selected_up_maps, preferred_element_type=jnp.float32
-    )
-    up_proj = jnp.dot(flattened, encoder_up_weight, preferred_element_type=jnp.float32).reshape(
-        requests, positions, -1
-    )
+    adapter_of_column = jnp.arange(tenant_adapters * rank, dtype=jnp.int32) // rank
+    low_rank = jnp.where(adapter[:, None] == adapter_of_column[None, :], low_rank, 0)
+    gated_hidden = jnp.dot(normed, encoder_gate_weight, preferred_element_type=jnp.float32)
+    gated_hidden = gated_hidden + adapter_scale * jnp.dot(
+        low_rank,
+        adapter_up_maps.reshape(tenant_adapters * rank, -1),
+        preferred_element_type=jnp.float32,
+    )
+    up_proj = jnp.dot(normed, encoder_up_weight, preferred_element_type=jnp.float32)
     hidden = (jax.nn.gelu(gated_hidden, approximate=True) * up_proj).astype(jnp.bfloat16)
     slots = jnp.arange(requests, dtype=jnp.int32)
     prompt_order = jnp.sum(
         slots[None, :] * (assignment[None, :] == slots[:, None]).astype(jnp.int32), axis=1
     )
-    source_row = prompt_order[my_slot]
-    live_length = lengths[source_row]
-    partial = jnp.einsum(
-        "rpf,fd->rpd", hidden, encoder_down_weight, preferred_element_type=jnp.float32
-    ).astype(jnp.bfloat16)
-    partial, full_image = tied(gather, partial, full_image)
-
-    summed = lax.psum_scatter(partial, "seq", scatter_dimension=2, tiled=True)
+    live_length = lengths[prompt_order[my_slot]]
+    partial = jnp.dot(hidden, encoder_down_weight, preferred_element_type=jnp.float32).astype(
+        jnp.bfloat16
+    )
+    (partial,) = tied(gather, partial)
+
+    summed = lax.psum_scatter(partial, "seq", scatter_dimension=1, tiled=True)
+    chosen, first = gather.pick(steps - 1)
+    waiting.append([chosen, gather.swap(chosen), first])
+    encoded = (summed.astype(jnp.float32) + tokens_in.astype(jnp.float32)).astype(jnp.bfloat16)
+    (encoded,) = tied(gather, encoded)
+
+    prompts = lax.all_gather(encoded, "heads", axis=0, tiled=True)
     gather.travel()
-    waiting = []
-    for step in range(1, steps - 1):
-        chosen, first = gather.pick(step)
-        waiting.append((chosen, gather.swap(chosen), first))
-    encoded = (
-        summed.astype(jnp.float32) + prompt_token_input.astype(jnp.float32)
-    ).astype(jnp.bfloat16)
-    (encoded,) = tied(gather, encoded)
-
-    prompts = lax.all_gather(encoded, "heads", axis=1, tiled=True)
-    gather.travel()
-    chosen, first = gather.pick(steps - 1)
-    waiting.append((chosen, gather.swap(chosen), first))
-    for chosen, theirs, first in waiting:
-        gather.keep(chosen, theirs, first)
-    text_count = prompts.shape[1]
-    ordered = jnp.take(prompts, prompt_order, axis=0).reshape(requests * text_count, -1)
+    text_count = positions
+    offsets = jnp.arange(text_count, dtype=jnp.int32)
+    rows = starts[prompt_order][:, None] + jnp.minimum(
+        offsets[None, :], lengths[prompt_order][:, None] - 1
+    )
+    ordered = jnp.take(prompts, rows.reshape(-1), axis=0, mode="clip")
     text_partial = (
         jnp.dot(ordered, text_weight, preferred_element_type=jnp.float32)
         .astype(jnp.bfloat16)
         .reshape(requests, text_count, -1)
     )
-    text_partial, gather.whole = tied(gather, text_partial, gather.whole)
+    flat = [item for chosen, theirs, _ in waiting for item in (chosen, *theirs)]
+    text_partial, full_image, *flat = tied(gather, text_partial, full_image, *flat)
+    for _, theirs, first in waiting:
+        gather.keep(flat[0], flat[1 : 1 + len(theirs)], first)
+        flat = flat[1 + len(theirs) :]
 
     text = lax.psum_scatter(text_partial, "seq", scatter_dimension=0, tiled=True)[0]
     chosen, first = gather.pick(steps)

time: 337 us -> 359 us (1.065)
  waiting for transfers between devices: 157 us -> 176 us
  local copies, waits for them, and re-layouts: 35.7 us -> 48.8 us
  matrix products: 65.9 us -> 55.7 us
  other arithmetic: 25.4 us -> 20.8 us
  starting transfers between devices: 17.9 us -> 21.9 us
    reduce_scatter x1, waiting for transfers between devices: 55.4 us -> 25.4 us  [local(): summed = lax.psum_scatter(partial, 'seq', scatter_dimension=1, tiled=True)]
    ppermute x3, waiting for transfers between devices: 48.2 us -> 70.2 us  [swap(): lax.ppermute(chosen, 'groups', [((i + turn) % self.replicas, i) for i in...]
    ppermute x3, waiting for transfers between devices: 4.19 us -> 17.1 us  [travel(): lax.ppermute(self.up[-1], 'seq', [(i, i + 1) for i in range(last)])]
    dot_general x5 -> x3, matrix products: 31.4 us -> 19.4 us  [the longest x1 11.6 us: local(): jnp.dot(hidden, encoder_down_weight, preferred_element_type=jnp.float32)]
    gather x1 -> x4, local copies, waits for them, and re-layouts: 2.27 us -> 12.3 us  [the longest x1 7.38 us: local(): ordered = jnp.take(prompts, rows.reshape(-1), axis=0, mode='clip')]
    ppermute x3, waiting for transfers between devices: 5.51 us -> 14.1 us  [travel(): lax.ppermute(self.down[-1], 'seq', [(i + 1, i) for i in range(last)])]
    all_gather x2 -> x3, waiting for transfers between devices: 40.3 us -> 48.7 us  [the longest x1 31.6 us: local(): whole = lax.all_gather(tokens_in, 'seq', axis=1, tiled=True)]
    dynamic_update_slice x3 -> x1, other arithmetic: 11.5 us -> 3.76 us  [put(): self.whole = lax.dynamic_update_slice_in_dim(self.whole, rows, first, 1)]
  transfers between devices with their start and end apart: 14 -> 15, of which waited for: 9 -> 10; matrix products, arithmetic and copies ran while one was open for 35% -> 31% of each run, Pallas kernels for 0% -> 0%
where the time goes in v3:
time: 359 us; the launch traced here: 358 us
  waiting for transfers between devices  176 us (49%)
  matrix products  55.7 us (16%)
  local copies, waits for them, and re-layouts  48.8 us (14%)
  starting transfers between devices  21.9 us (6%)
  other arithmetic  20.8 us (6%)
  between operations  18 us (5%)
  Pallas kernels  17.2 us (5%)
    ppermute x3, waiting for transfers between devices, swap(): lax.ppermute(chosen, 'groups', [((i + turn) % self.replicas, i) for i in...  70.2 us
    all_gather x1, waiting for transfers between devices, local(): whole = lax.all_gather(tokens_in, 'seq', axis=1, tiled=True)  31.6 us
    reduce_scatter x1, waiting for transfers between devices, local(): summed = lax.psum_scatter(partial, 'seq', scatter_dimension=1, tiled=True)  25.4 us
    dot_general x3, matrix products, local(): jnp.dot(full_image, gather.whole[j], preferred_element_type=jnp.float32)  22.1 us
    pallas_call x1, Pallas kernels, attention(): pl.pallas_call(functools.partial(attention_kernel, rows_per_step=rows_per...  17.2 us
    ppermute x3, waiting for transfers between devices, travel(): lax.ppermute(self.up[-1], 'seq', [(i, i + 1) for i in range(last)])  17.1 us
    all_gather x1, waiting for transfers between devices, local(): gathered = lax.all_gather(prompt_token_input, 'heads', axis=1, tiled=True)  17.1 us
    ppermute x3, waiting for transfers between devices, travel(): lax.ppermute(self.down[-1], 'seq', [(i + 1, i) for i in range(last)])  14.1 us
  transfers between devices with their start and end apart: 15, of which 10 were waited for; matrix products, arithmetic and copies ran while one was open for 31% of the time, Pallas kernels for 0%

profile of v3, /device:TPU:0, one launch (start us, length us, event | category | flops | bytes accessed | tf_op | source)
XLA Modules:
  0.0 358.3 jit_solution(4794925299039603147)
XLA Ops:
  6.6 3.1 dynamic-slice_bitcast_fusion
  9.7 1.3 collective-permute-start.1
  10.9 6.8 %collective-permute-start = (bf16[3,384,768]{2,1,0:T(8,128)(2,1)}, bf16[3,384,768]{2,1,0:T(8,128)(2,1)}, u32[]{:S(2)}, u32[]{:S(2)}) collective-permute-start(bf16[3,384,768]{2,1,0:T(8,128)(2,1)} %dynamic-slice_bitcast_fusion), channel_id=1, source_target_pairs={{0,4},{4,8},{8,12},{1,5},{5,9},{9,13},{2,6},{6,10},{10,14},{3,7},{... | collective-permute-start | bytes 5308424 | tf_op jit(solution)/shard_map/ppermute | solution.py:142
  17.8 0.2 reduce-window.8
  18.1 0.3 convert_reduce_fusion
  18.5 0.6 fusion.6
  19.1 0.8 copy-done.10
  19.9 2.2 copy.21
  22.2 1.9 fusion.9
  24.1 17.1 %all-gather.5.cloned.1.call-done = bf16[4,256,1024]{2,1,0:T(8,128)(2,1)} async-done(((bf16[4,64,1024]{2,1,0:T(8,128)(2,1)}), bf16[4,256,1024]{2,1,0:T(8,128)(2,1)}) %all-gather.5.cloned.1.call-update) | async-done | bytes 2097168 | tf_op jit(solution)/shard_map/all_gather | solution.py:202
  41.2 3.6 %gather_fusion = bf16[128,1024]{1,0:T(8,128)(2,1)} fusion(bf16[1024,1024]{1,0:T(8,128)(2,1)} %bitcast.99, s32[1024]{0:T(1024)S(1)} %pad_clamp_fusion.1), kind=kCustom, calls=%fused_computation | custom fusion | bytes 524800 | tf_op jit(solution)/shard_map/jit(_take)/gather | solution.py:219
  44.8 8.7 %collective-permute-done.1 = bf16[3,384,768]{2,1,0:T(8,128)(2,1)} collective-permute-done((bf16[3,384,768]{2,1,0:T(8,128)(2,1)}, bf16[3,384,768]{2,1,0:T(8,128)(2,1)}, u32[]{:S(2)}, u32[]{:S(2)}) %collective-permute-start.1) | collective-permute-done | bytes 1769504 | tf_op jit(solution)/shard_map/ppermute | solution.py:143
  53.5 1.2 collective-permute-done
  54.8 31.6 %all-gather.7.cloned.1.call-done = bf16[128,4096]{1,0:T(8,128)(2,1)} async-done(((bf16[128,1024]{1,0:T(8,128)(2,1)}), bf16[128,4096]{1,0:T(8,128)(2,1)}) %all-gather.7.cloned.1.call-update) | async-done | bytes 1048592 | tf_op jit(solution)/shard_map/all_gather | solution.py:231
  86.3 1.5 fusion.12
  87.9 4.8 %collective-permute-start.2 = (bf16[3,384,768]{2,1,0:T(8,128)(2,1)}, bf16[3,384,768]{2,1,0:T(8,128)(2,1)}, u32[]{:S(2)}, u32[]{:S(2)}) collective-permute-start(bf16[3,384,768]{2,1,0:T(8,128)(2,1)} %collective-permute-done), channel_id=1, source_target_pairs={{0,4},{4,8},{8,12},{1,5},{5,9},{9,13},{2,6},{6,10},{10,14},{3,7},{... | collective-permute-start | bytes 5308424 | tf_op jit(solution)/shard_map/ppermute | solution.py:142
  92.6 1.3 collective-permute-start.3
  93.9 5.9 %fusion.50 = f32[128,1280]{1,0:T(8,128)S(1)} fusion(bf16[4096,1280]{1,0:T(8,128)(2,1)} %param.21, bf16[128,4096]{1,0:T(8,128)(2,1)} %all-gather.7.cloned.1.call-done, f32[128]{0:T(128)S(1)} %add_rsqrt_fusion.1), kind=kOutput, calls=%fused_computation.100 | convolution fusion | flops 1343750144 | bytes 12190208 | tf_op jit(solution)/shard_map/dot_general | solution.py:250
  99.8 1.9 fusion.21
  101.8 11.6 %convolution_convert_fusion = bf16[128,4096]{1,0:T(8,128)(2,1)} fusion(bf16[1280,4096]{1,0:T(8,128)(2,1)} %param.23, f32[128,1280]{1,0:T(8,128)S(1)} %fusion.21, bf16[4096,1280]{1,0:T(8,128)(2,1)} %param.22, bf16[128,4096]{1,0:T(8,128)(2,1)S(1)} %copy-done.7, f32[128]{0:T(128)S(1)} %add_rsqrt_fusion.1), kind=kOutput, calls=%fused_computation.4 | convolution fusion | flops 2686779392 | bytes 23724544 | tf_op jit(solution)/shard_map/dot_general | solution.py:263
  113.4 15.9 %collective-permute-done.2 = bf16[3,384,768]{2,1,0:T(8,128)(2,1)} collective-permute-done((bf16[3,384,768]{2,1,0:T(8,128)(2,1)}, bf16[3,384,768]{2,1,0:T(8,128)(2,1)}, u32[]{:S(2)}, u32[]{:S(2)}) %collective-permute-start.2) | collective-permute-done | bytes 1769504 | tf_op jit(solution)/shard_map/ppermute | solution.py:142
  129.3 5.4 %collective-permute-done.3 = bf16[3,384,768]{2,1,0:T(8,128)(2,1)} collective-permute-done((bf16[3,384,768]{2,1,0:T(8,128)(2,1)}, bf16[3,384,768]{2,1,0:T(8,128)(2,1)}, u32[]{:S(2)}, u32[]{:S(2)}) %collective-permute-start.3) | collective-permute-done | bytes 1769504 | tf_op jit(solution)/shard_map/ppermute | solution.py:143
  134.8 25.4 %reduce-scatter.3.cloned.1.call-done = bf16[128,1024]{1,0:T(8,128)(2,1)} async-done(((bf16[128,4096]{1,0:T(8,128)(2,1)}), bf16[128,1024]{1,0:T(8,128)(2,1)}) %reduce-scatter.3.cloned.1.call-update) | async-done | bytes 262160 | tf_op jit(solution)/shard_map/reduce_scatter | solution.py:268
  160.2 1.7 add_convert_fusion
  162.0 0.5 all-gather.11.cloned.1.call-update
  162.6 0.7 dynamic_slice.26
  164.0 0.7 dynamic_slice.25
  165.3 0.7 dynamic_slice.24
  166.8 0.7 dynamic_slice.21
  168.8 4.1 %select_select_fusion.1 = (bf16[3,384,768]{2,1,0:T(8,128)(2,1)S(1)}, bf16[3,384,768]{2,1,0:T(8,128)(2,1)}) fusion(bf16[3,384,768]{2,1,0:T(8,128)(2,1)} %collective-permute-done.2, bf16[3,384,768]{2,1,0:T(8,128)(2,1)} %collective-permute-done.1, bf16[3,384,768]{2,1,0:T(8,128)(2,1)} %collective-permute-done, bf16[3,384,768]{2,1,0:T(8,128)(2,1)} %collective-permute-done.3, ...), kind=kLoop, calls=%fused_computation.31 | loop fusion | flops 3538944 | bytes 10616836 | tf_op jit(solution)/shard_map/jit(_where)/select_n | solution.py:157
  173.0 1.5 collective-permute-start.7
  174.4 0.6 collective-permute-start.6
  175.0 2.5 collective-permute-start.4
  177.5 1.5 collective-permute-start.5
  179.0 0.6 gather_fusion.1
  179.6 0.6 gather_fusion.2
  180.9 0.7 dynamic_slice.22.live_ref
  181.8 7.4 %gather_fusion.3 = bf16[1024,1024]{1,0:T(8,128)(2,1)} fusion(bf16[512,1024]{1,0:T(8,128)(2,1)} %all-gather.9.cloned.1.call-done, s32[1024]{0:T(1024)S(1)} %broadcast_clamp_fusion), kind=kCustom, calls=%fused_computation.3 | custom fusion | bytes 4198400 | tf_op jit(solution)/shard_map/jit(_take)/gather | solution.py:281
  189.1 7.8 %convolution_convert_fusion.1 = bf16[1024,1536]{1,0:T(8,128)(2,1)} fusion(bf16[1024,1024]{1,0:T(8,128)(2,1)} %gather_fusion.3, bf16[1024,1536]{1,0:T(8,128)(2,1)} %bitcast.97), kind=kOutput, calls=%fused_computation.13 | convolution fusion | flops 3222798336 | bytes 8388608 | tf_op jit(solution)/shard_map/dot_general | solution.py:283
  197.0 17.6 %collective-permute-done.7 = bf16[3,384,768]{2,1,0:T(8,128)(2,1)} collective-permute-done((bf16[3,384,768]{2,1,0:T(8,128)(2,1)S(1)}, bf16[3,384,768]{2,1,0:T(8,128)(2,1)}, u32[]{:S(2)}, u32[]{:S(2)}) %collective-permute-start.7) | collective-permute-done | bytes 1769504 | tf_op jit(solution)/shard_map/ppermute | solution.py:163
  214.6 36.6 %collective-permute-done.6 = bf16[3,384,768]{2,1,0:T(8,128)(2,1)} collective-permute-done((bf16[3,384,768]{2,1,0:T(8,128)(2,1)}, bf16[3,384,768]{2,1,0:T(8,128)(2,1)}, u32[]{:S(2)}, u32[]{:S(2)}) %collective-permute-start.6) | collective-permute-done | bytes 1769504 | tf_op jit(solution)/shard_map/ppermute | solution.py:163
  251.2 6.2 %broadcast_in_dim.33 = bf16[3,3072,768]{2,1,0:T(8,128)(2,1)} broadcast(bf16[]{:T(256)} %constant.88.clone.1), dimensions={} | broadcast | bytes 14155778 | tf_op jit(solution)/shard_map/broadcast_in_dim | solution.py:131
  257.4 4.1 %bitcast_dynamic-update-slice_fusion = bf16[3,3072,768]{2,1,0:T(8,128)(2,1)} fusion(bf16[3,3072,768]{2,1,0:T(8,128)(2,1)} %broadcast_in_dim.33, s32[]{:T(128)S(6)} %select_n.121, bf16[768,3,768]{2,0,1:T(8,128)(2,1)} %param.29), kind=kLoop, calls=%fused_computation.14 | loop fusion | bytes 7077892 | tf_op jit(solution)/shard_map/dynamic_update_slice | solution.py:138
  261.5 2.8 constant_dynamic-update-slice_fusion.4
  264.3 2.8 constant_dynamic-update-slice_fusion.3
  267.1 1.3 constant_dynamic-update-slice_fusion.2
  268.5 3.0 constant_dynamic-update-slice_fusion.1
  271.5 3.8 %constant_dynamic-update-slice_fusion = (bf16[3,3072,768]{2,1,0:T(8,128)(2,1)}, bf16[3,384,768]{2,1,0:T(8,128)(2,1)S(1)}) fusion(bf16[3,3072,768]{2,1,0:T(8,128)(2,1)} %constant_dynamic-update-slice_fusion.1, s32[]{:T(128)S(6)} %select_n.126, bf16[3,384,768]{2,1,0:T(8,128)(2,1)} %collective-permute-done.4, bf16[3,384,768]{2,1,0:T(8,128)(2,1)} %collective-permute-done.2, ...), kind=kLoop, calls=%fused_computation.77 | loop fusion | flops 2654208 | bytes 10616839 | tf_op jit(solution)/shard_map/dynamic_update_slice | solution.py:138
  275.2 1.5 collective-permute-start.8
  276.8 7.6 %fusion = f32[1024,768]{1,0:T(8,128)S(1)} fusion(bf16[1024,3072]{1,0:T(8,128)(2,1)S(1)} %bitcast.101, bf16[3,3072,768]{2,1,0:T(8,128)(2,1)} %get-tuple-element.61), kind=kOutput, calls=%fused_computation.6 | convolution fusion | flops 4831838208 | bytes 14155776 | tf_op jit(solution)/shard_map/dot_general | solution.py:298
  284.3 7.2 %fusion.1 = f32[1024,768]{1,0:T(8,128)S(1)} fusion(bf16[1024,3072]{1,0:T(8,128)(2,1)} %all-gather.11.cloned.1.call-done, bf16[3,3072,768]{2,1,0:T(8,128)(2,1)S(1)} %copy-done.9), kind=kOutput, calls=%fused_computation.8 | convolution fusion | flops 4831838208 | bytes 14155776 | tf_op jit(solution)/shard_map/dot_general | solution.py:298
  291.5 7.4 %fusion.2 = f32[1024,768]{1,0:T(8,128)S(1)} fusion(bf16[1024,3072]{1,0:T(8,128)(2,1)} %all-gather.11.cloned.1.call-done, bf16[3,3072,768]{2,1,0:T(8,128)(2,1)S(1)} %copy-done.9), kind=kOutput, calls=%fused_computation.10 | convolution fusion | flops 4831838208 | bytes 14155776 | tf_op jit(solution)/shard_map/dot_general | solution.py:298
  298.9 16.0 %collective-permute-done.8 = bf16[3,384,768]{2,1,0:T(8,128)(2,1)S(1)} collective-permute-done((bf16[3,384,768]{2,1,0:T(8,128)(2,1)S(1)}, bf16[3,384,768]{2,1,0:T(8,128)(2,1)S(1)}, u32[]{:S(2)}, u32[]{:S(2)}) %collective-permute-start.8) | collective-permute-done | bytes 1769504 | tf_op jit(solution)/shard_map/ppermute | solution.py:163
  314.9 2.1 fusion.22
  317.0 2.1 add.239.value_ref
  319.1 2.1 fusion.26
  321.2 2.0 add.237.query_ref
  323.2 2.1 fusion.24
  325.3 2.1 add.238.key_ref
  327.5 1.9 copy-done.2
  329.4 1.9 copy-done.3
  331.2 1.9 copy-done.4
  333.1 1.1 copy-done.5
  334.3 17.2 %shard_map.163 = bf16[1024,768]{1,0:T(8,128)(2,1)} custom-call(s32[1]{0:T(128)} %dynamic_slice.22.live_ref, f32[6,3,128]{2,1,0:T(4,128)S(1)} %bitcast.92, f32[1024,768]{1,0:T(8,128)S(1)} %copy-done.3, f32[1024,768]{1,0:T(8,128)S(1)} %copy-done.4, f32[1024,768]{1,0:T(8,128)S(1)} %copy-done.2, bf16[256,1536]{1,0:T(8,128)(2,1)S(1)} %bitcast.93, ...), custom_call_target="tpu_custom_call" | custom-call | flops 4026531840 | bytes 11796480 | tf_op jit(solution)/shard_map/pallas_call | solution.py:87
  (75 shorter events, 0.9 us)
Async XLA Ops:
  6.5 93.3 %copy-start = (bf16[8,4096,16]{1,2,0:T(8,128)(2,1)S(1)}, bf16[8,4096,16]{1,2,0:T(8,128)(2,1)}, u32[]{:S(2)}) copy-start(bf16[8,4096,16]{1,2,0:T(8,128)(2,1)} %param.24) | copy-start | bytes 3145732
  6.5 11.3 %copy-start.6 = (s32[4]{0:T(128)S(1)}, s32[4]{0:T(128)}, u32[]{:S(2)}) copy-start(s32[4]{0:T(128)} %param.18) | copy-start | bytes 52
  6.5 11.6 %copy-start.8 = (bf16[1,256,3072]{2,1,0:T(8,128)(2,1)S(1)}, bf16[1,256,3072]{2,1,0:T(8,128)(2,1)}, u32[]{:S(2)}) copy-start(bf16[1,256,3072]{2,1,0:T(8,128)(2,1)} %param.27) | copy-start | bytes 4718596
  6.5 11.9 %copy-start.14 = (s32[4]{0:T(128)S(1)}, s32[4]{0:T(128)}, u32[]{:S(2)}) copy-start(s32[4]{0:T(128)} %param.19) | copy-start | bytes 52
  6.5 34.6 %all-gather.5.cloned.1.call-start = ((), (), s32[]{:S(2)}) async-start(), calls=%async_computation.2 | async-start | bytes 2621440 | tf_op jit(solution)/shard_map/all_gather | solution.py:202
  6.6 12.5 %copy-start.12 = (bf16[1,2,3072]{2,1,0:T(2,128)(2,1)S(1)}, bf16[1,2,3072]{2,1,0:T(2,128)(2,1)}, u32[]{:S(2)}) copy-start(bf16[1,2,3072]{2,1,0:T(2,128)(2,1)} %param.28) | copy-start | bytes 36868
  9.7 43.8 %collective-permute-start.1 = (bf16[3,384,768]{2,1,0:T(8,128)(2,1)}, bf16[3,384,768]{2,1,0:T(8,128)(2,1)}, u32[]{:S(2)}, u32[]{:S(2)}) collective-permute-start(bf16[3,384,768]{2,1,0:T(8,128)(2,1)} %dynamic-slice_bitcast_fusion), channel_id=1, source_target_pairs={{4,0},{8,4},{12,8},{5,1},{9,5},{13,9},{6,2},{10,6},{14,10},{7,3},{... | collective-permute-start | bytes 5308424 | tf_op jit(solution)/shard_map/ppermute | solution.py:143
  10.9 43.7 %collective-permute-start = (bf16[3,384,768]{2,1,0:T(8,128)(2,1)}, bf16[3,384,768]{2,1,0:T(8,128)(2,1)}, u32[]{:S(2)}, u32[]{:S(2)}) collective-permute-start(bf16[3,384,768]{2,1,0:T(8,128)(2,1)} %dynamic-slice_bitcast_fusion), channel_id=1, source_target_pairs={{0,4},{4,8},{8,12},{1,5},{5,9},{9,13},{2,6},{6,10},{10,14},{3,7},{... | collective-permute-start | bytes 5308424 | tf_op jit(solution)/shard_map/ppermute | solution.py:142
  17.8 68.5 %all-gather.7.cloned.1.call-start = ((), (), s32[]{:S(2)}) async-start(), calls=%async_computation.3 | async-start | bytes 1310720 | tf_op jit(solution)/shard_map/all_gather | solution.py:231
  18.0 1.9 copy-start.10
  54.7 105.5 %reduce-scatter.3.cloned.1.call-start = ((), (), s32[]{:S(2)}) async-start(), calls=%async_computation.4 | async-start | bytes 1310720 | tf_op jit(solution)/shard_map/reduce_scatter | solution.py:268
  87.9 12.0 %copy-start.7 = (bf16[128,4096]{1,0:T(8,128)(2,1)S(1)}, bf16[128,4096]{1,0:T(8,128)(2,1)}, u32[]{:S(2)}) copy-start(bf16[128,4096]{1,0:T(8,128)(2,1)} %all-gather.7.cloned.1.call-done) | copy-start | bytes 3145732
  87.9 41.4 %collective-permute-start.2 = (bf16[3,384,768]{2,1,0:T(8,128)(2,1)}, bf16[3,384,768]{2,1,0:T(8,128)(2,1)}, u32[]{:S(2)}, u32[]{:S(2)}) collective-permute-start(bf16[3,384,768]{2,1,0:T(8,128)(2,1)} %collective-permute-done), channel_id=1, source_target_pairs={{0,4},{4,8},{8,12},{1,5},{5,9},{9,13},{2,6},{6,10},{10,14},{3,7},{... | collective-permute-start | bytes 5308424 | tf_op jit(solution)/shard_map/ppermute | solution.py:142
  92.6 42.0 %collective-permute-start.3 = (bf16[3,384,768]{2,1,0:T(8,128)(2,1)}, bf16[3,384,768]{2,1,0:T(8,128)(2,1)}, u32[]{:S(2)}, u32[]{:S(2)}) collective-permute-start(bf16[3,384,768]{2,1,0:T(8,128)(2,1)} %collective-permute-done.1), channel_id=1, source_target_pairs={{4,0},{8,4},{12,8},{5,1},{9,5},{13,9},{6,2},{10,6},{14,10},{7,3},{... | collective-permute-start | bytes 5308424 | tf_op jit(solution)/shard_map/ppermute | solution.py:143
  101.8 58.4 %copy-start.11 = (bf16[128,1024]{1,0:T(8,128)(2,1)S(1)}, bf16[128,1024]{1,0:T(8,128)(2,1)}, u32[]{:S(2)}) copy-start(bf16[128,1024]{1,0:T(8,128)(2,1)} %gather_fusion) | copy-start | bytes 786436
  113.4 49.2 %copy-start.18 = (s32[4]{0:T(128)S(1)}, s32[4]{0:T(128)}, u32[]{:S(2)}) copy-start(s32[4]{0:T(128)} %constant.97.clone) | copy-start | bytes 52
  113.4 50.6 %copy-start.17 = (s32[4]{0:T(128)S(1)}, s32[4]{0:T(128)}, u32[]{:S(2)}) copy-start(s32[4]{0:T(128)} %constant.96.clone) | copy-start | bytes 52
  113.4 51.9 %copy-start.16 = (s32[4]{0:T(128)S(1)}, s32[4]{0:T(128)}, u32[]{:S(2)}) copy-start(s32[4]{0:T(128)} %constant.95.clone) | copy-start | bytes 52
  113.4 53.3 %copy-start.15 = (s32[4]{0:T(128)S(1)}, s32[4]{0:T(128)}, u32[]{:S(2)}) copy-start(s32[4]{0:T(128)} %param.20) | copy-start | bytes 52
  134.7 47.0 %all-gather.9.cloned.1.call-start = ((), (), s32[]{:S(2)}) async-start(), calls=%async_computation.5 | async-start | bytes 1310720 | tf_op jit(solution)/shard_map/all_gather | solution.py:274
  161.9 89.3 %all-gather.11.cloned.1.call-start = ((), (), s32[]{:S(2)}) async-start(), calls=%async_computation.6 | async-start | bytes 7864320 | tf_op jit(solution)/shard_map/all_gather | solution.py:234
  162.5 164.9 %reduce-scatter.5.cloned.1.call-start = ((), (), s32[]{:S(2)}) async-start(), calls=%async_computation.7 | async-start | bytes 3932160 | tf_op jit(solution)/shard_map/reduce_scatter | solution.py:293
  168.8 12.8 %copy-start.13 = (f32[3,6,128]{2,1,0:T(8,128)S(1)}, f32[3,6,128]{2,1,0:T(8,128)}, u32[]{:S(2)}) copy-start(f32[3,6,128]{2,1,0:T(8,128)} %param.30) | copy-start | bytes 27652
  173.0 41.6 %collective-permute-start.7 = (bf16[3,384,768]{2,1,0:T(8,128)(2,1)S(1)}, bf16[3,384,768]{2,1,0:T(8,128)(2,1)}, u32[]{:S(2)}, u32[]{:S(2)}) collective-permute-start(bf16[3,384,768]{2,1,0:T(8,128)(2,1)S(1)} %get-tuple-element.52), channel_id=1, source_target_pairs={{16,0},{0,16},{17,1},{1,17},{18,2},{2,18},{19,3},{3,19},{20,4},{4,... | collective-permute-start | bytes 5308424 | tf_op jit(solution)/shard_map/ppermute | solution.py:163
  174.4 76.7 %collective-permute-start.6 = (bf16[3,384,768]{2,1,0:T(8,128)(2,1)}, bf16[3,384,768]{2,1,0:T(8,128)(2,1)}, u32[]{:S(2)}, u32[]{:S(2)}) collective-permute-start(bf16[3,384,768]{2,1,0:T(8,128)(2,1)} %get-tuple-element.50), channel_id=1, source_target_pairs={{16,0},{0,16},{17,1},{1,17},{18,2},{2,18},{19,3},{3,19},{20,4},{4,... | collective-permute-start | bytes 5308424 | tf_op jit(solution)/shard_map/ppermute | solution.py:163
  175.0 76.2 %collective-permute-start.4 = (bf16[3,384,768]{2,1,0:T(8,128)(2,1)}, bf16[3,384,768]{2,1,0:T(8,128)(2,1)}, u32[]{:S(2)}, u32[]{:S(2)}) collective-permute-start(bf16[3,384,768]{2,1,0:T(8,128)(2,1)} %collective-permute-done.2), channel_id=1, source_target_pairs={{0,4},{4,8},{8,12},{1,5},{5,9},{9,13},{2,6},{6,10},{10,14},{3,7},{... | collective-permute-start | bytes 5308424 | tf_op jit(solution)/shard_map/ppermute | solution.py:142
  177.5 73.7 %collective-permute-start.5 = (bf16[3,384,768]{2,1,0:T(8,128)(2,1)}, bf16[3,384,768]{2,1,0:T(8,128)(2,1)}, u32[]{:S(2)}, u32[]{:S(2)}) collective-permute-start(bf16[3,384,768]{2,1,0:T(8,128)(2,1)} %collective-permute-done.3), channel_id=1, source_target_pairs={{4,0},{8,4},{12,8},{5,1},{9,5},{13,9},{6,2},{10,6},{14,10},{7,3},{... | collective-permute-start | bytes 5308424 | tf_op jit(solution)/shard_map/ppermute | solution.py:143
  268.5 8.3 %slice-start = ((s8[6291456]{0:T(1024)(128)(4,1)}), s8[4194304]{0:T(1024)(128)(4,1)S(1)}, s32[]{:S(2)}) async-start(s8[6291456]{0:T(1024)(128)(4,1)} %bitcast.100), calls=%async_computation.8 | async-start | bytes 8388608
  271.5 5.3 %slice-start.1 = ((s8[6291456]{0:T(1024)(128)(4,1)}), s8[2097152]{0:T(1024)(128)(4,1)S(1)}, s32[]{:S(2)}) async-start(s8[6291456]{0:T(1024)(128)(4,1)} %bitcast.100), calls=%async_computation.9 | async-start | bytes 4194304
  275.2 39.7 %collective-permute-start.8 = (bf16[3,384,768]{2,1,0:T(8,128)(2,1)S(1)}, bf16[3,384,768]{2,1,0:T(8,128)(2,1)S(1)}, u32[]{:S(2)}, u32[]{:S(2)}) collective-permute-start(bf16[3,384,768]{2,1,0:T(8,128)(2,1)S(1)} %get-tuple-element.62), channel_id=1, source_target_pairs={{16,0},{0,16},{17,1},{1,17},{18,2},{2,18},{19,3},{3,19},{20,4},{4,... | collective-permute-start | bytes 5308424 | tf_op jit(solution)/shard_map/ppermute | solution.py:163
  276.8 7.6 %copy-start.9 = (bf16[3,3072,768]{2,1,0:T(8,128)(2,1)S(1)}, bf16[3,3072,768]{2,1,0:T(8,128)(2,1)}, u32[]{:S(2)}) copy-start(bf16[3,3072,768]{2,1,0:T(8,128)(2,1)} %get-tuple-element.61) | copy-start | bytes 42467332
  327.5 1.9 copy-start.2
  329.4 1.9 copy-start.3
  331.2 1.9 copy-start.4
  333.1 1.1 copy-start.5
  334.3 17.2 %copy-start.1 = (bf16[8,4096,16]{1,2,0:T(8,128)(2,1)S(1)}, bf16[8,4096,16]{1,2,0:T(8,128)(2,1)}, u32[]{:S(2)}) copy-start(bf16[8,4096,16]{1,2,0:T(8,128)(2,1)} %param.24) | copy-start | bytes 3145732
Sparse Core Ops, SparseCore 0:
  17.9 23.2 all-gather.4
  54.8 31.4 all-gather.6
  134.8 25.2 reduce-scatter.2
  162.1 15.3 all-gather.8
  178.9 46.3 all-gather.10
  251.3 59.5 reduce-scatter.4

commit v4 on v3

--- a/solution.py
+++ b/solution.py
@@ -229,7 +229,7 @@
     tokens_in, modulated, text_weight = tied(gather, tokens_in, modulated, text_weight)
 
     whole = lax.all_gather(tokens_in, "seq", axis=1, tiled=True)
-    whole, modulated = tied(gather, whole, modulated)
+    whole, modulated, gather.whole = tied(gather, whole, modulated, gather.whole)
 
     full_image = lax.all_gather(modulated, "heads", axis=0, tiled=True)
     waiting = []
@@ -263,13 +263,15 @@
     partial = jnp.dot(hidden, encoder_down_weight, preferred_element_type=jnp.float32).astype(
         jnp.bfloat16
     )
-    (partial,) = tied(gather, partial)
+    partial, full_image, waiting = tied(gather, partial, full_image, waiting)
+    for chosen, theirs, first in waiting:
+        gather.keep(chosen, theirs, first)
 
     summed = lax.psum_scatter(partial, "seq", scatter_dimension=1, tiled=True)
     chosen, first = gather.pick(steps - 1)
-    waiting.append([chosen, gather.swap(chosen), first])
+    theirs = gather.swap(chosen)
     encoded = (summed.astype(jnp.float32) + tokens_in.astype(jnp.float32)).astype(jnp.bfloat16)
-    (encoded,) = tied(gather, encoded)
+    encoded, gather.whole = tied(gather, encoded, gather.whole)
 
     prompts = lax.all_gather(encoded, "heads", axis=0, tiled=True)
     gather.travel()
@@ -284,11 +286,8 @@
         .astype(jnp.bfloat16)
         .reshape(requests, text_count, -1)
     )
-    flat = [item for chosen, theirs, _ in waiting for item in (chosen, *theirs)]
-    text_partial, full_image, *flat = tied(gather, text_partial, full_image, *flat)
-    for _, theirs, first in waiting:
-        gather.keep(flat[0], flat[1 : 1 + len(theirs)], first)
-        flat = flat[1 + len(theirs) :]
+    text_partial, chosen, theirs = tied(gather, text_partial, chosen, theirs)
+    gather.keep(chosen, theirs, first)
 
     text = lax.psum_scatter(text_partial, "seq", scatter_dimension=0, tiled=True)[0]
     chosen, first = gather.pick(steps)

time: 359 us -> 312 us (0.87)
  waiting for transfers between devices: 176 us -> 116 us
  local copies, waits for them, and re-layouts: 48.8 us -> 62.4 us
    ppermute x3, waiting for transfers between devices: 70.2 us -> 47.4 us  [swap(): lax.ppermute(chosen, 'groups', [((i + turn) % self.replicas, i) for i in...]
    reduce_scatter x1, waiting for transfers between devices: 25.4 us -> 7.94 us  [local(): summed = lax.psum_scatter(partial, 'seq', scatter_dimension=1, tiled=True)]
    ppermute x3, waiting for transfers between devices: 17.1 us -> 1.66 us  [travel(): lax.ppermute(self.up[-1], 'seq', [(i, i + 1) for i in range(last)])]
    dynamic_update_slice x5, local copies, waits for them, and re-layouts: 14.1 us -> 28.4 us  [put(): self.whole = lax.dynamic_update_slice_in_dim(self.whole, rows, first, 1)]
    all_gather x1, waiting for transfers between devices: 31.6 us -> 21.5 us  [local(): whole = lax.all_gather(tokens_in, 'seq', axis=1, tiled=True)]
    all_gather x1, waiting for transfers between devices: 0.02 us -> 6.62 us  [local(): prompts = lax.all_gather(encoded, 'heads', axis=0, tiled=True)]
  transfers between devices with their start and end apart: 15 -> 15, of which waited for: 10 -> 11; matrix products, arithmetic and copies ran while one was open for 31% -> 40% of each run, Pallas kernels for 0% -> 0%
where the time goes in v4:
time: 312 us; the launch traced here: 311 us
  waiting for transfers between devices  116 us (37%)
  local copies, waits for them, and re-layouts  62.4 us (20%)
  matrix products  55.2 us (18%)
  starting transfers between devices  21.8 us (7%)
  other arithmetic  20.3 us (7%)
  between operations  17.6 us (6%)
  Pallas kernels  17 us (5%)
    ppermute x3, waiting for transfers between devices, swap(): lax.ppermute(chosen, 'groups', [((i + turn) % self.replicas, i) for i in...  47.4 us
    dynamic_update_slice x5, local copies, waits for them, and re-layouts, put(): self.whole = lax.dynamic_update_slice_in_dim(self.whole, rows, first, 1)  28.4 us
    dot_general x3, matrix products, local(): jnp.dot(full_image, gather.whole[j], preferred_element_type=jnp.float32)  22 us
    all_gather x1, waiting for transfers between devices, local(): whole = lax.all_gather(tokens_in, 'seq', axis=1, tiled=True)  21.5 us
    pallas_call x1, Pallas kernels, attention(): pl.pallas_call(functools.partial(attention_kernel, rows_per_step=rows_per...  17 us
    all_gather x1, waiting for transfers between devices, local(): gathered = lax.all_gather(prompt_token_input, 'heads', axis=1, tiled=True)  17 us
    ppermute x3, waiting for transfers between devices, travel(): lax.ppermute(self.down[-1], 'seq', [(i + 1, i) for i in range(last)])  14 us
    ppermute x3, starting transfers between devices, travel(): lax.ppermute(self.up[-1], 'seq', [(i, i + 1) for i in range(last)])  14 us
  transfers between devices with their start and end apart: 15, of which 11 were waited for; matrix products, arithmetic and copies ran while one was open for 40% of the time, Pallas kernels for 0%

profile of v4, /device:TPU:0, one launch (start us, length us, event | category | flops | bytes accessed | tf_op | source)
XLA Modules:
  0.0 310.6 jit_solution(14934993867305957440)
XLA Ops:
  6.6 3.0 dynamic-slice_bitcast_fusion
  9.6 1.3 collective-permute-start.1
  10.8 6.9 %collective-permute-start = (bf16[3,384,768]{2,1,0:T(8,128)(2,1)}, bf16[3,384,768]{2,1,0:T(8,128)(2,1)}, u32[]{:S(2)}, u32[]{:S(2)}) collective-permute-start(bf16[3,384,768]{2,1,0:T(8,128)(2,1)} %dynamic-slice_bitcast_fusion), channel_id=1, source_target_pairs={{0,4},{4,8},{8,12},{1,5},{5,9},{9,13},{2,6},{6,10},{10,14},{3,7},{... | collective-permute-start | bytes 5308424 | tf_op jit(solution)/shard_map/ppermute | solution.py:142
  18.1 0.3 convert_reduce_fusion
  18.5 0.6 fusion.6
  19.1 0.8 copy-done.10
  19.9 2.2 copy.21
  22.2 1.9 fusion.9
  24.1 17.0 %all-gather.5.cloned.1.call-done = bf16[4,256,1024]{2,1,0:T(8,128)(2,1)} async-done(((bf16[4,64,1024]{2,1,0:T(8,128)(2,1)}), bf16[4,256,1024]{2,1,0:T(8,128)(2,1)}) %all-gather.5.cloned.1.call-update) | async-done | bytes 2097168 | tf_op jit(solution)/shard_map/all_gather | solution.py:202
  41.1 3.6 %gather_fusion = bf16[128,1024]{1,0:T(8,128)(2,1)} fusion(bf16[1024,1024]{1,0:T(8,128)(2,1)} %bitcast.99, s32[1024]{0:T(1024)S(1)} %pad_clamp_fusion.1), kind=kCustom, calls=%fused_computation | custom fusion | bytes 524800 | tf_op jit(solution)/shard_map/jit(_take)/gather | solution.py:219
  44.7 8.7 %collective-permute-done.1 = bf16[3,384,768]{2,1,0:T(8,128)(2,1)} collective-permute-done((bf16[3,384,768]{2,1,0:T(8,128)(2,1)}, bf16[3,384,768]{2,1,0:T(8,128)(2,1)}, u32[]{:S(2)}, u32[]{:S(2)}) %collective-permute-start.1) | collective-permute-done | bytes 1769504 | tf_op jit(solution)/shard_map/ppermute | solution.py:143
  53.4 1.2 collective-permute-done
  54.7 6.0 %broadcast_in_dim.31 = bf16[3,3072,768]{2,1,0:T(8,128)(2,1)} broadcast(bf16[]{:T(256)} %constant.84.clone.1), dimensions={} | broadcast | bytes 14155778 | tf_op jit(solution)/shard_map/broadcast_in_dim | solution.py:131
  60.6 4.1 %bitcast_dynamic-update-slice_fusion = bf16[3,3072,768]{2,1,0:T(8,128)(2,1)} fusion(bf16[3,3072,768]{2,1,0:T(8,128)(2,1)} %broadcast_in_dim.31, s32[]{:T(128)S(6)} %select_n.107, bf16[768,3,768]{2,0,1:T(8,128)(2,1)} %param.29), kind=kLoop, calls=%fused_computation.14 | loop fusion | bytes 7077892 | tf_op jit(solution)/shard_map/dynamic_update_slice | solution.py:138
  64.7 21.5 %all-gather.7.cloned.1.call-done = bf16[128,4096]{1,0:T(8,128)(2,1)} async-done(((bf16[128,1024]{1,0:T(8,128)(2,1)}), bf16[128,4096]{1,0:T(8,128)(2,1)}) %all-gather.7.cloned.1.call-update) | async-done | bytes 1048592 | tf_op jit(solution)/shard_map/all_gather | solution.py:231
  86.3 0.6 dynamic_slice.24
  87.5 4.6 %collective-permute-start.2 = (bf16[3,384,768]{2,1,0:T(8,128)(2,1)}, bf16[3,384,768]{2,1,0:T(8,128)(2,1)}, u32[]{:S(2)}, u32[]{:S(2)}) collective-permute-start(bf16[3,384,768]{2,1,0:T(8,128)(2,1)} %collective-permute-done), channel_id=1, source_target_pairs={{0,4},{4,8},{8,12},{1,5},{5,9},{9,13},{2,6},{6,10},{10,14},{3,7},{... | collective-permute-start | bytes 5308424 | tf_op jit(solution)/shard_map/ppermute | solution.py:142
  92.1 1.3 collective-permute-start.3
  93.4 3.1 broadcast_select_fusion
  96.5 1.5 collective-permute-start.4
  98.0 0.3 fusion.12
  98.3 5.7 %fusion.50 = f32[128,1280]{1,0:T(8,128)S(1)} fusion(bf16[4096,1280]{1,0:T(8,128)(2,1)} %param.21, bf16[128,4096]{1,0:T(8,128)(2,1)S(1)} %copy-done.7, f32[128]{0:T(128)S(1)} %add_rsqrt_fusion.1), kind=kOutput, calls=%fused_computation.98 | convolution fusion | flops 1343750144 | bytes 12190208 | tf_op jit(solution)/shard_map/dot_general | solution.py:250
  103.9 1.9 fusion.21
  105.9 11.7 %convolution_convert_fusion = bf16[128,4096]{1,0:T(8,128)(2,1)} fusion(bf16[1280,4096]{1,0:T(8,128)(2,1)} %param.23, f32[128,1280]{1,0:T(8,128)S(1)} %fusion.21, bf16[4096,1280]{1,0:T(8,128)(2,1)} %param.22, bf16[128,4096]{1,0:T(8,128)(2,1)S(1)} %copy-done.7, f32[128]{0:T(128)S(1)} %add_rsqrt_fusion.1), kind=kOutput, calls=%fused_computation.4 | convolution fusion | flops 2686779392 | bytes 23724544 | tf_op jit(solution)/shard_map/dot_general | solution.py:263
  117.6 19.1 %collective-permute-done.4 = bf16[3,384,768]{2,1,0:T(8,128)(2,1)} collective-permute-done((bf16[3,384,768]{2,1,0:T(8,128)(2,1)}, bf16[3,384,768]{2,1,0:T(8,128)(2,1)}, u32[]{:S(2)}, u32[]{:S(2)}) %collective-permute-start.4) | collective-permute-done | bytes 1769504 | tf_op jit(solution)/shard_map/ppermute | solution.py:163
  136.8 10.0 %dynamic_update_slice.19 = bf16[3,3072,768]{2,1,0:T(8,128)(2,1)} dynamic-update-slice(bf16[3,3072,768]{2,1,0:T(8,128)(2,1)} %bitcast_dynamic-update-slice_fusion, bf16[3,384,768]{2,1,0:T(8,128)(2,1)} %broadcast_select_fusion, s32[]{:T(128)} %constant.31.clone.1, s32[]{:T(128)S(6)} %select_n.113, s32[]{:T(128)} %constant.31.clone.1) | dynamic-update-slice | bytes 3538948 | tf_op jit(solution)/shard_map/dynamic_update_slice | solution.py:138
  146.8 9.9 %dynamic_update_slice.20 = bf16[3,3072,768]{2,1,0:T(8,128)(2,1)} dynamic-update-slice(bf16[3,3072,768]{2,1,0:T(8,128)(2,1)} %dynamic_update_slice.19, bf16[3,384,768]{2,1,0:T(8,128)(2,1)} %collective-permute-done.4, s32[]{:T(128)} %constant.31.clone.1, s32[]{:T(128)S(6)} %select_n.114, s32[]{:T(128)} %constant.31.clone.1) | dynamic-update-slice | bytes 3538948 | tf_op jit(solution)/shard_map/dynamic_update_slice | solution.py:138
  156.7 7.9 %reduce-scatter.3.cloned.1.call-done = bf16[128,1024]{1,0:T(8,128)(2,1)} async-done(((bf16[128,4096]{1,0:T(8,128)(2,1)}), bf16[128,1024]{1,0:T(8,128)(2,1)}) %reduce-scatter.3.cloned.1.call-update) | async-done | bytes 262160 | tf_op jit(solution)/shard_map/reduce_scatter | solution.py:270
  164.7 1.7 add_convert_fusion
  166.8 1.8 select_select_fusion.1
  168.6 1.5 collective-permute-start.7
  170.1 2.5 collective-permute-start.5
  172.6 1.3 collective-permute-start.6
  173.9 0.6 gather_fusion.1
  174.6 0.6 gather_fusion.2
  175.3 6.6 %all-gather.11.cloned.1.call-done = bf16[512,1024]{1,0:T(8,128)(2,1)} async-done(((bf16[128,1024]{1,0:T(8,128)(2,1)}), bf16[512,1024]{1,0:T(8,128)(2,1)}) %all-gather.11.cloned.1.call-update) | async-done | bytes 1048592 | tf_op jit(solution)/shard_map/all_gather | solution.py:276
  181.9 7.4 %gather_fusion.3 = bf16[1024,1024]{1,0:T(8,128)(2,1)} fusion(bf16[512,1024]{1,0:T(8,128)(2,1)} %all-gather.11.cloned.1.call-done, s32[1024]{0:T(1024)S(1)} %broadcast_clamp_fusion), kind=kCustom, calls=%fused_computation.3 | custom fusion | bytes 4198400 | tf_op jit(solution)/shard_map/jit(_take)/gather | solution.py:283
  189.3 7.6 %convolution_convert_fusion.1 = bf16[1024,1536]{1,0:T(8,128)(2,1)} fusion(bf16[1024,1024]{1,0:T(8,128)(2,1)} %gather_fusion.3, bf16[1024,1536]{1,0:T(8,128)(2,1)} %bitcast.97), kind=kOutput, calls=%fused_computation.13 | convolution fusion | flops 3222798336 | bytes 8388608 | tf_op jit(solution)/shard_map/dot_general | solution.py:285
  196.9 12.0 %collective-permute-done.7 = bf16[3,384,768]{2,1,0:T(8,128)(2,1)} collective-permute-done((bf16[3,384,768]{2,1,0:T(8,128)(2,1)S(1)}, bf16[3,384,768]{2,1,0:T(8,128)(2,1)}, u32[]{:S(2)}, u32[]{:S(2)}) %collective-permute-start.7) | collective-permute-done | bytes 1769504 | tf_op jit(solution)/shard_map/ppermute | solution.py:163
  208.9 0.5 collective-permute-done.5
  209.4 5.3 %collective-permute-done.6 = bf16[3,384,768]{2,1,0:T(8,128)(2,1)} collective-permute-done((bf16[3,384,768]{2,1,0:T(8,128)(2,1)}, bf16[3,384,768]{2,1,0:T(8,128)(2,1)}, u32[]{:S(2)}, u32[]{:S(2)}) %collective-permute-start.6) | collective-permute-done | bytes 1769504 | tf_op jit(solution)/shard_map/ppermute | solution.py:143
  214.7 0.6 dynamic_slice.26
  216.0 0.6 dynamic_slice.25
  217.2 0.6 dynamic_slice.21
  219.8 0.6 dynamic_slice.22.live_ref
  220.4 1.4 constant_dynamic-update-slice_fusion.2
  221.7 3.0 constant_dynamic-update-slice_fusion.1
  224.7 3.8 %constant_dynamic-update-slice_fusion = (bf16[3,3072,768]{2,1,0:T(8,128)(2,1)}, bf16[3,384,768]{2,1,0:T(8,128)(2,1)S(1)}) fusion(bf16[3,3072,768]{2,1,0:T(8,128)(2,1)} %constant_dynamic-update-slice_fusion.1, s32[]{:T(128)S(6)} %select_n.126, bf16[3,384,768]{2,1,0:T(8,128)(2,1)} %collective-permute-done.5, bf16[3,384,768]{2,1,0:T(8,128)(2,1)} %collective-permute-done.2, ...), kind=kLoop, calls=%fused_computation.79 | loop fusion | flops 2654208 | bytes 10616839 | tf_op jit(solution)/shard_map/dynamic_update_slice | solution.py:138
  228.5 0.6 collective-permute-start.8
  229.1 7.6 %fusion = f32[1024,768]{1,0:T(8,128)S(1)} fusion(bf16[1024,3072]{1,0:T(8,128)(2,1)S(1)} %bitcast.101, bf16[3,3072,768]{2,1,0:T(8,128)(2,1)} %get-tuple-element.67), kind=kOutput, calls=%fused_computation.6 | convolution fusion | flops 4831838208 | bytes 14155776 | tf_op jit(solution)/shard_map/dot_general | solution.py:297
  236.6 7.1 %fusion.1 = f32[1024,768]{1,0:T(8,128)S(1)} fusion(bf16[1024,3072]{1,0:T(8,128)(2,1)} %all-gather.9.cloned.1.call-done, bf16[3,3072,768]{2,1,0:T(8,128)(2,1)S(1)} %copy-done.9), kind=kOutput, calls=%fused_computation.8 | convolution fusion | flops 4831838208 | bytes 14155776 | tf_op jit(solution)/shard_map/dot_general | solution.py:297
  243.8 7.4 %fusion.2 = f32[1024,768]{1,0:T(8,128)S(1)} fusion(bf16[1024,3072]{1,0:T(8,128)(2,1)} %all-gather.9.cloned.1.call-done, bf16[3,3072,768]{2,1,0:T(8,128)(2,1)S(1)} %copy-done.9), kind=kOutput, calls=%fused_computation.10 | convolution fusion | flops 4831838208 | bytes 14155776 | tf_op jit(solution)/shard_map/dot_general | solution.py:297
  251.1 16.3 %collective-permute-done.8 = bf16[3,384,768]{2,1,0:T(8,128)(2,1)S(1)} collective-permute-done((bf16[3,384,768]{2,1,0:T(8,128)(2,1)S(1)}, bf16[3,384,768]{2,1,0:T(8,128)(2,1)S(1)}, u32[]{:S(2)}, u32[]{:S(2)}) %collective-permute-start.8) | collective-permute-done | bytes 1769504 | tf_op jit(solution)/shard_map/ppermute | solution.py:163
  267.4 2.1 fusion.22
  269.5 2.1 add.239.value_ref
  271.6 2.1 fusion.26
  273.7 2.1 add.237.query_ref
  275.8 2.1 fusion.24
  277.9 2.1 add.238.key_ref
  279.9 1.9 copy-done.2
  281.8 1.9 copy-done.3
  283.7 1.9 copy-done.4
  285.6 1.1 copy-done.5
  286.7 17.0 %shard_map.163 = bf16[1024,768]{1,0:T(8,128)(2,1)} custom-call(s32[1]{0:T(128)} %dynamic_slice.22.live_ref, f32[6,3,128]{2,1,0:T(4,128)S(1)} %bitcast.92, f32[1024,768]{1,0:T(8,128)S(1)} %copy-done.3, f32[1024,768]{1,0:T(8,128)S(1)} %copy-done.4, f32[1024,768]{1,0:T(8,128)S(1)} %copy-done.2, bf16[256,1536]{1,0:T(8,128)(2,1)S(1)} %bitcast.93, ...), custom_call_target="tpu_custom_call" | custom-call | flops 4026531840 | bytes 11796480 | tf_op jit(solution)/shard_map/pallas_call | solution.py:87
  (76 shorter events, 1.3 us)
Async XLA Ops:
  6.5 97.4 %copy-start = (bf16[8,4096,16]{1,2,0:T(8,128)(2,1)S(1)}, bf16[8,4096,16]{1,2,0:T(8,128)(2,1)}, u32[]{:S(2)}) copy-start(bf16[8,4096,16]{1,2,0:T(8,128)(2,1)} %param.24) | copy-start | bytes 3145732
  6.5 11.3 %copy-start.6 = (s32[4]{0:T(128)S(1)}, s32[4]{0:T(128)}, u32[]{:S(2)}) copy-start(s32[4]{0:T(128)} %param.18) | copy-start | bytes 52
  6.5 11.5 %copy-start.8 = (bf16[1,256,3072]{2,1,0:T(8,128)(2,1)S(1)}, bf16[1,256,3072]{2,1,0:T(8,128)(2,1)}, u32[]{:S(2)}) copy-start(bf16[1,256,3072]{2,1,0:T(8,128)(2,1)} %param.27) | copy-start | bytes 4718596
  6.5 11.8 %copy-start.14 = (s32[4]{0:T(128)S(1)}, s32[4]{0:T(128)}, u32[]{:S(2)}) copy-start(s32[4]{0:T(128)} %param.19) | copy-start | bytes 52
  6.5 34.5 %all-gather.5.cloned.1.call-start = ((), (), s32[]{:S(2)}) async-start(), calls=%async_computation.2 | async-start | bytes 2621440 | tf_op jit(solution)/shard_map/all_gather | solution.py:202
  6.6 12.4 %copy-start.12 = (bf16[1,2,3072]{2,1,0:T(2,128)(2,1)S(1)}, bf16[1,2,3072]{2,1,0:T(2,128)(2,1)}, u32[]{:S(2)}) copy-start(bf16[1,2,3072]{2,1,0:T(2,128)(2,1)} %param.28) | copy-start | bytes 36868
  9.6 43.8 %collective-permute-start.1 = (bf16[3,384,768]{2,1,0:T(8,128)(2,1)}, bf16[3,384,768]{2,1,0:T(8,128)(2,1)}, u32[]{:S(2)}, u32[]{:S(2)}) collective-permute-start(bf16[3,384,768]{2,1,0:T(8,128)(2,1)} %dynamic-slice_bitcast_fusion), channel_id=1, source_target_pairs={{4,0},{8,4},{12,8},{5,1},{9,5},{13,9},{6,2},{10,6},{14,10},{7,3},{... | collective-permute-start | bytes 5308424 | tf_op jit(solution)/shard_map/ppermute | solution.py:143
  10.8 43.7 %collective-permute-start = (bf16[3,384,768]{2,1,0:T(8,128)(2,1)}, bf16[3,384,768]{2,1,0:T(8,128)(2,1)}, u32[]{:S(2)}, u32[]{:S(2)}) collective-permute-start(bf16[3,384,768]{2,1,0:T(8,128)(2,1)} %dynamic-slice_bitcast_fusion), channel_id=1, source_target_pairs={{0,4},{4,8},{8,12},{1,5},{5,9},{9,13},{2,6},{6,10},{10,14},{3,7},{... | collective-permute-start | bytes 5308424 | tf_op jit(solution)/shard_map/ppermute | solution.py:142
  17.7 68.5 %all-gather.7.cloned.1.call-start = ((), (), s32[]{:S(2)}) async-start(), calls=%async_computation.3 | async-start | bytes 1310720 | tf_op jit(solution)/shard_map/all_gather | solution.py:231
  18.0 1.9 copy-start.10
  54.6 82.1 %all-gather.9.cloned.1.call-start = ((), (), s32[]{:S(2)}) async-start(), calls=%async_computation.4 | async-start | bytes 7864320 | tf_op jit(solution)/shard_map/all_gather | solution.py:234
  60.6 25.7 %copy-start.18 = (s32[4]{0:T(128)S(1)}, s32[4]{0:T(128)}, u32[]{:S(2)}) copy-start(s32[4]{0:T(128)} %constant.95.clone) | copy-start | bytes 52
  86.2 11.7 %copy-start.7 = (bf16[128,4096]{1,0:T(8,128)(2,1)S(1)}, bf16[128,4096]{1,0:T(8,128)(2,1)}, u32[]{:S(2)}) copy-start(bf16[128,4096]{1,0:T(8,128)(2,1)} %all-gather.7.cloned.1.call-done) | copy-start | bytes 3145732
  86.3 78.4 %reduce-scatter.3.cloned.1.call-start = ((), (), s32[]{:S(2)}) async-start(), calls=%async_computation.5 | async-start | bytes 1310720 | tf_op jit(solution)/shard_map/reduce_scatter | solution.py:270
  87.5 49.2 %collective-permute-start.2 = (bf16[3,384,768]{2,1,0:T(8,128)(2,1)}, bf16[3,384,768]{2,1,0:T(8,128)(2,1)}, u32[]{:S(2)}, u32[]{:S(2)}) collective-permute-start(bf16[3,384,768]{2,1,0:T(8,128)(2,1)} %collective-permute-done), channel_id=1, source_target_pairs={{0,4},{4,8},{8,12},{1,5},{5,9},{9,13},{2,6},{6,10},{10,14},{3,7},{... | collective-permute-start | bytes 5308424 | tf_op jit(solution)/shard_map/ppermute | solution.py:142
  92.1 44.5 %collective-permute-start.3 = (bf16[3,384,768]{2,1,0:T(8,128)(2,1)}, bf16[3,384,768]{2,1,0:T(8,128)(2,1)}, u32[]{:S(2)}, u32[]{:S(2)}) collective-permute-start(bf16[3,384,768]{2,1,0:T(8,128)(2,1)} %collective-permute-done.1), channel_id=1, source_target_pairs={{4,0},{8,4},{12,8},{5,1},{9,5},{13,9},{6,2},{10,6},{14,10},{7,3},{... | collective-permute-start | bytes 5308424 | tf_op jit(solution)/shard_map/ppermute | solution.py:143
  96.5 40.1 %collective-permute-start.4 = (bf16[3,384,768]{2,1,0:T(8,128)(2,1)}, bf16[3,384,768]{2,1,0:T(8,128)(2,1)}, u32[]{:S(2)}, u32[]{:S(2)}) collective-permute-start(bf16[3,384,768]{2,1,0:T(8,128)(2,1)} %broadcast_select_fusion), channel_id=1, source_target_pairs={{16,0},{0,16},{17,1},{1,17},{18,2},{2,18},{19,3},{3,19},{20,4},{4,... | collective-permute-start | bytes 5308424 | tf_op jit(solution)/shard_map/ppermute | solution.py:163
  136.7 45.2 %all-gather.11.cloned.1.call-start = ((), (), s32[]{:S(2)}) async-start(), calls=%async_computation.6 | async-start | bytes 1310720 | tf_op jit(solution)/shard_map/all_gather | solution.py:276
  136.8 27.9 %copy-start.11 = (bf16[128,1024]{1,0:T(8,128)(2,1)S(1)}, bf16[128,1024]{1,0:T(8,128)(2,1)}, u32[]{:S(2)}) copy-start(bf16[128,1024]{1,0:T(8,128)(2,1)} %gather_fusion) | copy-start | bytes 786436
  146.8 19.8 %copy-start.15 = (s32[4]{0:T(128)S(1)}, s32[4]{0:T(128)}, u32[]{:S(2)}) copy-start(s32[4]{0:T(128)} %param.20) | copy-start | bytes 52
  166.4 113.5 %reduce-scatter.5.cloned.1.call-start = ((), (), s32[]{:S(2)}) async-start(), calls=%async_computation.7 | async-start | bytes 3932160 | tf_op jit(solution)/shard_map/reduce_scatter | solution.py:292
  168.6 40.3 %collective-permute-start.7 = (bf16[3,384,768]{2,1,0:T(8,128)(2,1)S(1)}, bf16[3,384,768]{2,1,0:T(8,128)(2,1)}, u32[]{:S(2)}, u32[]{:S(2)}) collective-permute-start(bf16[3,384,768]{2,1,0:T(8,128)(2,1)S(1)} %select_select_fusion.1), channel_id=1, source_target_pairs={{16,0},{0,16},{17,1},{1,17},{18,2},{2,18},{19,3},{3,19},{20,4},{4,... | collective-permute-start | bytes 5308424 | tf_op jit(solution)/shard_map/ppermute | solution.py:163
  170.1 39.3 %collective-permute-start.5 = (bf16[3,384,768]{2,1,0:T(8,128)(2,1)}, bf16[3,384,768]{2,1,0:T(8,128)(2,1)}, u32[]{:S(2)}, u32[]{:S(2)}) collective-permute-start(bf16[3,384,768]{2,1,0:T(8,128)(2,1)} %collective-permute-done.2), channel_id=1, source_target_pairs={{0,4},{4,8},{8,12},{1,5},{5,9},{9,13},{2,6},{6,10},{10,14},{3,7},{... | collective-permute-start | bytes 5308424 | tf_op jit(solution)/shard_map/ppermute | solution.py:142
  172.6 42.1 %collective-permute-start.6 = (bf16[3,384,768]{2,1,0:T(8,128)(2,1)}, bf16[3,384,768]{2,1,0:T(8,128)(2,1)}, u32[]{:S(2)}, u32[]{:S(2)}) collective-permute-start(bf16[3,384,768]{2,1,0:T(8,128)(2,1)} %collective-permute-done.3), channel_id=1, source_target_pairs={{4,0},{8,4},{12,8},{5,1},{9,5},{13,9},{6,2},{10,6},{14,10},{7,3},{... | collective-permute-start | bytes 5308424 | tf_op jit(solution)/shard_map/ppermute | solution.py:143
  196.9 17.8 %copy-start.17 = (s32[4]{0:T(128)S(1)}, s32[4]{0:T(128)}, u32[]{:S(2)}) copy-start(s32[4]{0:T(128)} %constant.97.clone) | copy-start | bytes 52
  196.9 19.0 %copy-start.16 = (s32[4]{0:T(128)S(1)}, s32[4]{0:T(128)}, u32[]{:S(2)}) copy-start(s32[4]{0:T(128)} %constant.96.clone) | copy-start | bytes 52
  196.9 23.4 %copy-start.13 = (f32[3,6,128]{2,1,0:T(8,128)S(1)}, f32[3,6,128]{2,1,0:T(8,128)}, u32[]{:S(2)}) copy-start(f32[3,6,128]{2,1,0:T(8,128)} %param.30) | copy-start | bytes 27652
  221.7 7.3 %slice-start = ((s8[6291456]{0:T(1024)(128)(4,1)}), s8[4194304]{0:T(1024)(128)(4,1)S(1)}, s32[]{:S(2)}) async-start(s8[6291456]{0:T(1024)(128)(4,1)} %bitcast.100), calls=%async_computation.8 | async-start | bytes 8388608
  224.7 4.3 %slice-start.1 = ((s8[6291456]{0:T(1024)(128)(4,1)}), s8[2097152]{0:T(1024)(128)(4,1)S(1)}, s32[]{:S(2)}) async-start(s8[6291456]{0:T(1024)(128)(4,1)} %bitcast.100), calls=%async_computation.9 | async-start | bytes 4194304
  228.5 38.9 %collective-permute-start.8 = (bf16[3,384,768]{2,1,0:T(8,128)(2,1)S(1)}, bf16[3,384,768]{2,1,0:T(8,128)(2,1)S(1)}, u32[]{:S(2)}, u32[]{:S(2)}) collective-permute-start(bf16[3,384,768]{2,1,0:T(8,128)(2,1)S(1)} %get-tuple-element.68), channel_id=1, source_target_pairs={{16,0},{0,16},{17,1},{1,17},{18,2},{2,18},{19,3},{3,19},{20,4},{4,... | collective-permute-start | bytes 5308424 | tf_op jit(solution)/shard_map/ppermute | solution.py:163
  229.1 7.6 %copy-start.9 = (bf16[3,3072,768]{2,1,0:T(8,128)(2,1)S(1)}, bf16[3,3072,768]{2,1,0:T(8,128)(2,1)}, u32[]{:S(2)}) copy-start(bf16[3,3072,768]{2,1,0:T(8,128)(2,1)} %get-tuple-element.67) | copy-start | bytes 42467332
  279.9 1.9 copy-start.2
  281.8 1.9 copy-start.3
  283.7 1.9 copy-start.4
  285.6 1.1 copy-start.5
  286.7 17.1 %copy-start.1 = (bf16[8,4096,16]{1,2,0:T(8,128)(2,1)S(1)}, bf16[8,4096,16]{1,2,0:T(8,128)(2,1)}, u32[]{:S(2)}) copy-start(bf16[8,4096,16]{1,2,0:T(8,128)(2,1)} %param.24) | copy-start | bytes 3145732
Sparse Core Ops, SparseCore 0:
  17.9 23.1 all-gather.4
  54.7 31.4 all-gather.6
  87.8 45.8 all-gather.8
  136.8 27.7 reduce-scatter.2
  166.5 15.3 all-gather.10
  214.8 58.4 reduce-scatter.4
